TPU v7x, 32 devices: a whole 2x2x4 slice. The times are simulated.
32 devices in a mesh: parts: 2 (over x), seq: 16 (over z, y, core).
Axes of the slice: x: 2, y: 2, z: 4, core: 2. Of those that a mesh axis runs over, the one named last changes fastest.
Arguments:
- proj_main: bfloat16 [2, 4096, 4096], P(None, ('parts', 'seq')), parts along dimension 1, may hold values from -6 to 6
- proj_state: bfloat16 [2, 4096, 128], P(None, ('parts', 'seq')), parts along dimension 1, may hold values from -6 to 6
- step_raw: float32 [2, 4096, 16], P(None, ('parts', 'seq')), parts along dimension 1, may hold values from -0.5 to 1.5
- step_bias: float32 [16], replicated, may hold values from -6.5 to -5.5
- decay_log: float32 [16], replicated, may hold values from -10 to 3
- skip_scale: float32 [16], replicated, may hold values from 0.5 to 2
- norm_gain: float32 [2048], replicated, may hold values from 0.1 to 1.9
- out_weight: bfloat16 [2048, 1024], P('seq'), may hold values from -0.125 to 0.125
- grad_mixed: bfloat16 [4096, 1024], P(('parts', 'seq')), parts along dimension 0, may hold values from -6 to 6
Outputs:
- mixed_out: bfloat16 [4096, 1024], P(('parts', 'seq')), parts along dimension 0
- grad_main: bfloat16 [2, 4096, 4096], P(None, ('parts', 'seq')), parts along dimension 1
- grad_state: float32 [2, 4096, 128], P(None, ('parts', 'seq')), parts along dimension 1
- grad_step: float32 [2, 4096, 16], P(None, ('parts', 'seq')), parts along dimension 1
- grad_weight: float32 [4096, 1024], P(('parts', 'seq')), parts along dimension 0
There are 2 independent parts, one for each index of `parts`. A program takes and returns all parts, laid end to end along the dimension named above; an argument that names none is the same for every part. Nothing has to cross between parts.
All inputs are finite; a program needn't handle non-finite values.
Results may differ from a plain program's by a relative error of at most 0.0059.
Values may be sent and summed in bfloat16 or wider, within the bound.
A program may use at most 128 MiB of HBM per device.

v0:
```python
import jax
import jax.numpy as jnp
from jax import lax
from jax.sharding import PartitionSpec as P

D = 1024
HEADS = 16
HEAD_DIM = 128
STATE = 64
BLOCK = 128
INNER = 2048


PRECISE = lax.Precision.HIGHEST
EPSILON = 1e-05


def from_behind(x, axis, by):
    length = lax.axis_size(axis)
    pairs = [(i, i + by) for i in range(length) if 0 <= i + by < length]
    return lax.ppermute(x, axis, pairs)


def from_partner(block, axis, stride):
    count = lax.axis_size(axis)
    route = []
    for low in range(count):
        high = low | 1 << stride
        if high != low and high < count:
            route += [(low, high), (high, low)]
    return lax.ppermute(block, axis, route)


def block_step(carry_state, block_data):
    x_part, b_part, c_part, rate_part, step_part = block_data
    cumulative = jnp.cumsum(rate_part, axis=0)
    positions = jnp.arange(rate_part.shape[0])
    lower_mask = (positions[:, None] >= positions[None, :])[:, :, None]
    gaps_log = cumulative[:, None, :] - cumulative[None, :, :]
    decay_mat = jnp.where(lower_mask, jnp.exp(jnp.where(lower_mask, gaps_log, 0.0)), 0.0)
    scores = jnp.dot(c_part, b_part.T, precision=PRECISE)
    mixing = scores[:, :, None] * decay_mat * step_part[None, :, :]
    inside = jnp.einsum("tuh,uhp->thp", mixing, x_part, precision=PRECISE)
    carried = jnp.exp(cumulative)[:, :, None] * jnp.einsum(
        "tn,hpn->thp", c_part, carry_state, precision=PRECISE
    )
    weighting = jnp.exp(cumulative[-1][None, :] - cumulative) * step_part
    fresh = jnp.einsum("uhp,un->hpn", weighting[:, :, None] * x_part, b_part, precision=PRECISE)
    next_state = jnp.exp(cumulative[-1])[:, None, None] * carry_state + fresh
    return (next_state, inside + carried)


def strand_scan(x_vals, b_vals, c_vals, rate_vals, step_vals, block_len):
    blocks_count = x_vals.shape[0] // block_len
    pieces_all = tuple(
        (
            array_in.reshape((blocks_count, block_len) + array_in.shape[1:])
            for array_in in (x_vals, b_vals, c_vals, rate_vals, step_vals)
        )
    )
    zero_state = jnp.zeros((x_vals.shape[1], x_vals.shape[2], b_vals.shape[1]), x_vals.dtype)
    last_state, outputs = lax.scan(block_step, zero_state, pieces_all)
    return (outputs.reshape(x_vals.shape), last_state)


def strand_core(x_vals, b_vals, c_vals, step_raw, step_bias, decay_log, skip_scale):
    step_vals = jax.nn.softplus(step_raw + step_bias)
    rate_vals = -jnp.exp(decay_log) * step_vals
    y_local, last_state = strand_scan(x_vals, b_vals, c_vals, rate_vals, step_vals, BLOCK)
    cumulative = jnp.cumsum(rate_vals, axis=0)
    return (y_local + skip_scale[:, None] * x_vals, last_state, cumulative[-1], cumulative)


def gate_norm(y_vals, z_vals, norm_gain):
    flat_y = y_vals.reshape(y_vals.shape[0], -1)
    gated = flat_y * jax.nn.silu(z_vals)
    return gated * lax.rsqrt(jnp.mean(gated * gated, axis=-1, keepdims=True) + EPSILON) * norm_gain


def combine(earlier, latter):
    return (earlier[0] * latter[0], latter[0][..., None, None] * earlier[1] + latter[1])


def carried_term(cumulative, c_vals, entering):
    return jnp.exp(cumulative)[..., None] * jnp.einsum(
        "stn,shpn->sthp", c_vals, entering, precision=PRECISE
    )


def pass_forward(values):
    levels = lax.axis_size("seq").bit_length() - 1
    running = values
    for round_index in range(levels + 1):
        distance = 1 if round_index == 0 else 2 ** (round_index - 1)
        arrived = from_behind((running[0], running[1]), "seq", distance)
        running = arrived if round_index == 0 else combine(arrived, running)
    return running[1]


def pass_backward(values):
    levels = lax.axis_size("seq").bit_length() - 1
    running = values
    for round_index in range(levels + 1):
        distance = 1 if round_index == 0 else 2 ** (round_index - 1)
        arrived = from_behind((running[0], running[1]), "seq", -distance)
        running = arrived if round_index == 0 else combine(arrived, running)
    return running[1]


def mirror(first_block, second_block):
    seq_count = lax.axis_size("seq")
    moved_first, moved_second = (first_block, second_block)
    for bit_index in range(seq_count.bit_length() - 1):
        moved_first, moved_second = from_partner((moved_first, moved_second), "seq", bit_index)
    return (moved_first[::-1, ::-1], moved_second[::-1, ::-1])


def per_device(
    proj_main,
    proj_state,
    step_raw,
    step_bias,
    decay_log,
    skip_scale,
    norm_gain,
    out_weight,
    grad_mixed,
):
    local_rows = proj_main.shape[1]
    x_vals = proj_main[:, :, :INNER].astype(jnp.float32).reshape(2, local_rows, HEADS, HEAD_DIM)
    z_vals = proj_main[:, :, INNER:].astype(jnp.float32)
    b_vals = proj_state[:, :, :STATE].astype(jnp.float32)
    c_vals = proj_state[:, :, STATE:].astype(jnp.float32)

    def local_core(x_in, b_in, c_in, raw_in):
        return jax.vmap(
            lambda x_one, b_one, c_one, raw_one: strand_core(
                x_one, b_one, c_one, raw_one, step_bias, decay_log, skip_scale
            )
        )(x_in, b_in, c_in, raw_in)

    (y_local, state_local, log_decay, cumulative), core_back = jax.vjp(
        local_core, x_vals, b_vals, c_vals, step_raw
    )
    decay_total = jnp.exp(log_decay)
    entering = pass_forward((decay_total, state_local))
    carried, carried_back = jax.vjp(carried_term, cumulative, c_vals, entering)
    y_vals = y_local + carried

    def norm_fn(y_in, z_in):
        return jax.vmap(gate_norm, in_axes=(0, 0, None))(y_in, z_in, norm_gain)

    normed, norm_back = jax.vjp(norm_fn, y_vals, z_vals)
    normed_rows = normed.astype(jnp.bfloat16).reshape(2 * local_rows, INNER)
    whole_weight = lax.all_gather(out_weight, "seq", axis=0, tiled=True)
    out_rows = jnp.dot(normed_rows, whole_weight, preferred_element_type=jnp.float32)
    strand_out = out_rows.astype(jnp.bfloat16).reshape(2, local_rows, D)
    mirrored_out, mirrored_grad = mirror(strand_out[1], grad_mixed)
    mixed_out = (strand_out[0].astype(jnp.float32) + mirrored_out.astype(jnp.float32)).astype(
        jnp.bfloat16
    )
    backward_in = jnp.stack([grad_mixed, mirrored_grad]).reshape(2 * local_rows, D)
    grad_weight = lax.psum_scatter(
        jnp.einsum("re,rd->ed", normed_rows, backward_in, preferred_element_type=jnp.float32),
        "seq",
        scatter_dimension=0,
        tiled=True,
    )
    grad_normed = jnp.einsum(
        "rd,ed->re", backward_in, whole_weight, preferred_element_type=jnp.float32
    )
    grad_y, grad_z = norm_back(grad_normed.reshape(2, local_rows, INNER))
    grad_cumul, grad_c_carried, grad_entering = carried_back(grad_y)
    leaving = pass_backward((decay_total, grad_entering))
    grad_log = decay_total * jnp.sum(leaving * entering, axis=(-2, -1))
    grad_x, grad_b, grad_c_local, grad_step = core_back((grad_y, leaving, grad_log, grad_cumul))
    grad_main = jnp.concatenate([grad_x.reshape(2, local_rows, INNER), grad_z], axis=-1).astype(
        jnp.bfloat16
    )
    grad_state = jnp.concatenate([grad_b, grad_c_local + grad_c_carried], axis=-1)
    return (mixed_out, grad_main, grad_state, grad_step, grad_weight)


def solution(mesh):
    placed = (
        P(None, ("parts", "seq"), None),
        P(None, ("parts", "seq"), None),
        P(None, ("parts", "seq"), None),
        P(),
        P(),
        P(),
        P(),
        P("seq", None),
        P(("parts", "seq"), None),
    )
    return jax.shard_map(
        per_device,
        mesh=mesh,
        in_specs=placed,
        out_specs=(
            P(("parts", "seq"), None),
            P(None, ("parts", "seq"), None),
            P(None, ("parts", "seq"), None),
            P(None, ("parts", "seq"), None),
            P(("parts", "seq"), None),
        ),
        check_vma=False,
    )
```

profile of v0, /device:TPU:0, one launch (start us, length us, event | category | flops | bytes accessed | tf_op | source)
XLA Modules:
  0.0 454.8 jit_solution(6768569895222457781)
XLA Ops:
  11.8 2.4 collective-permute-start.4
  14.2 2.2 collective-permute-done.4
  16.4 16.9 %collective-permute-start.5 = (f32[2,16,128,64]{2,3,1,0:T(8,128)S(1)}, f32[2,16,128,64]{2,3,1,0:T(8,128)S(1)}, u32[]{:S(2)}, u32[]{:S(2)}) collective-permute-start(f32[2,16,128,64]{2,3,1,0:T(8,128)S(1)} %collective-permute-done.4), channel_id=1, source_target_pairs={{0,1},{1,2},{2,3},{3,4},{4,5},{5,6},{6,7},{7,8},{8,9},{9,10},{10,1... | collective-permute-start | bytes 3145736 | tf_op jit(solution)/shard_map/ppermute | solution.py:21
  33.3 4.3 collective-permute-start
  38.6 24.8 %collective-permute-start.6 = (f32[2,16,128,64]{2,3,1,0:T(8,128)S(1)}, f32[2,16,128,64]{2,3,1,0:T(8,128)S(1)}, u32[]{:S(2)}, u32[]{:S(2)}) collective-permute-start(f32[2,16,128,64]{2,3,1,0:T(8,128)S(1)} %multiply_add_fusion.7), channel_id=1, source_target_pairs={{0,2},{1,3},{2,4},{3,5},{4,6},{5,7},{6,8},{7,9},{8,10},{9,11},{10,... | collective-permute-start | bytes 3145736 | tf_op jit(solution)/shard_map/ppermute | solution.py:21
  63.3 11.4 %collective-permute-start.1 = (f32[2,16]{1,0:T(2,128)S(1)}, f32[2,16]{1,0:T(2,128)S(1)}, u32[]{:S(2)}, u32[]{:S(2)}) collective-permute-start(f32[2,16]{1,0:T(2,128)S(1)} %collective-permute-done), channel_id=1, source_target_pairs={{0,1},{1,2},{2,3},{3,4},{4,5},{5,6},{6,7},{7,8},{8,9},{9,10},{10,1... | collective-permute-start | bytes 392 | tf_op jit(solution)/shard_map/ppermute | solution.py:21
  75.6 2.3 collective-permute-done.6
  78.1 21.9 %collective-permute-start.7 = (f32[2,16,128,64]{2,3,1,0:T(8,128)S(1)}, f32[2,16,128,64]{2,3,1,0:T(8,128)S(1)}, u32[]{:S(2)}, u32[]{:S(2)}) collective-permute-start(f32[2,16,128,64]{2,3,1,0:T(8,128)S(1)} %multiply_add_fusion.6), channel_id=1, source_target_pairs={{0,4},{1,5},{2,6},{3,7},{4,8},{5,9},{6,10},{7,11},{8,12},{9,13},{1... | collective-permute-start | bytes 3145736 | tf_op jit(solution)/shard_map/ppermute | solution.py:21
  100.0 3.6 collective-permute-start.2
  105.0 15.6 %collective-permute-done.7 = f32[2,16,128,64]{2,3,1,0:T(8,128)S(1)} collective-permute-done((f32[2,16,128,64]{2,3,1,0:T(8,128)S(1)}, f32[2,16,128,64]{2,3,1,0:T(8,128)S(1)}, u32[]{:S(2)}, u32[]{:S(2)}) %collective-permute-start.7) | collective-permute-done | bytes 1048608 | tf_op jit(solution)/shard_map/ppermute | solution.py:21
  120.7 8.3 %collective-permute-start.8 = (f32[2,16,128,64]{2,3,1,0:T(8,128)S(1)}, f32[2,16,128,64]{2,3,1,0:T(8,128)}, u32[]{:S(2)}, u32[]{:S(2)}) collective-permute-start(f32[2,16,128,64]{2,3,1,0:T(8,128)S(1)} %multiply_add_fusion.5), channel_id=1, source_target_pairs={{0,8},{1,9},{2,10},{3,11},{4,12},{5,13},{6,14},{7,15},{16,24},{17,... | collective-permute-start | bytes 3145736 | tf_op jit(solution)/shard_map/ppermute | solution.py:21
  129.6 5.8 %collective-permute-done.14 = bf16[128,1024]{1,0:T(8,128)(2,1)S(1)} collective-permute-done((bf16[128,1024]{1,0:T(8,128)(2,1)S(1)}, bf16[128,1024]{1,0:T(8,128)(2,1)S(1)}, u32[]{:S(2)}, u32[]{:S(2)}) %collective-permute-start.14) | collective-permute-done | bytes 262176 | tf_op jit(solution)/shard_map/ppermute | solution.py:31
  136.8 20.0 %collective-permute-done.15 = bf16[128,1024]{1,0:T(8,128)(2,1)S(1)} collective-permute-done((bf16[128,1024]{1,0:T(8,128)(2,1)S(1)}, bf16[128,1024]{1,0:T(8,128)(2,1)S(1)}, u32[]{:S(2)}, u32[]{:S(2)}) %collective-permute-start.15) | collective-permute-done | bytes 262176 | tf_op jit(solution)/shard_map/ppermute | solution.py:31
  156.7 2.4 fusion.71
  159.1 4.5 collective-permute-start.3
  166.8 3.0 rev.7
  171.2 1.9 fusion.81
  173.1 4.2 fusion.9
  177.3 1.9 copy.50
  179.3 4.7 %multiply_reduce_fusion.1 = (f32[2,128]{1,0:T(2,128)S(1)}, f32[2,128]{1,0:T(2,128)S(1)}, f32[2,128,2048]{2,1,0:T(8,128)S(1)}, f32[2,128,2048]{2,1,0:T(8,128)S(1)}) fusion(f32[2,128,2048]{2,1,0:T(8,128)S(1)} %copy.50, bf16[2,128,4096]{2,1,0:T(8,128)(2,1)} %param.9, f32[2048]{0:T(1024)} %param.15, bf16[2048,1024]{1,0:T(8,128)(2,1)} %all-gather.2.cloned.1.call-done, ...), kind=kOutput, calls=%fused_computation.39 | convolution fusion | flops 1079770624 | bytes 12068864 | tf_op jit(solution)/shard_map/rd,ed->re/dot_general | solution.py:169
  184.0 2.8 fusion.68
  187.8 4.6 %convolution_bitcast_fusion = f32[2048,1024]{1,0:T(8,128)} fusion(bf16[2,128,2048]{2,1,0:T(8,128)(2,1)S(1)} %get-tuple-element.376, bf16[1,128,1024]{2,1,0:T(8,128)(2,1)S(1)} %bitcast.133, bf16[1,128,1024]{2,1,0:T(8,128)(2,1)S(1)} %bitcast.135), kind=kOutput, calls=%fused_computation | convolution fusion | flops 1074003968 | bytes 9961472 | tf_op jit(solution)/shard_map/re,rd->ed/dot_general | solution.py:164
  192.4 1.9 copy.51
  197.1 3.3 collective-permute-done.21
  203.0 12.4 %collective-permute-done.17 = f32[2,16]{1,0:T(2,128)S(1)} collective-permute-done((f32[2,16]{1,0:T(2,128)S(1)}, f32[2,16]{1,0:T(2,128)S(1)}, u32[]{:S(2)}, u32[]{:S(2)}) %collective-permute-start.17) | collective-permute-done | bytes 160 | tf_op jit(solution)/shard_map/ppermute | solution.py:21
  215.5 1.6 collective-permute-start.23
  218.5 12.9 %collective-permute-done.18 = f32[2,16]{1,0:T(2,128)S(1)} collective-permute-done((f32[2,16]{1,0:T(2,128)S(1)}, f32[2,16]{1,0:T(2,128)S(1)}, u32[]{:S(2)}, u32[]{:S(2)}) %collective-permute-start.18) | collective-permute-done | bytes 160 | tf_op jit(solution)/shard_map/ppermute | solution.py:21
  232.7 28.1 %collective-permute-done.19 = f32[2,16]{1,0:T(2,128)S(1)} collective-permute-done((f32[2,16]{1,0:T(2,128)S(1)}, f32[2,16]{1,0:T(2,128)S(1)}, u32[]{:S(2)}, u32[]{:S(2)}) %collective-permute-start.19) | collective-permute-done | bytes 160 | tf_op jit(solution)/shard_map/ppermute | solution.py:21
  262.8 45.3 %collective-permute-done.20 = f32[2,16]{1,0:T(2,128)S(1)} collective-permute-done((f32[2,16]{1,0:T(2,128)S(1)}, f32[2,16]{1,0:T(2,128)S(1)}, u32[]{:S(2)}, u32[]{:S(2)}) %collective-permute-start.20) | collective-permute-done | bytes 160 | tf_op jit(solution)/shard_map/ppermute | solution.py:21
  308.8 1.5 collective-permute-start.24
  312.5 4.1 fusion.50
  316.6 2.4 collective-permute-start.10
  319.9 10.8 %collective-permute-done.10 = bf16[128,1024]{1,0:T(8,128)(2,1)S(1)} collective-permute-done((bf16[128,1024]{1,0:T(8,128)(2,1)S(1)}, bf16[128,1024]{1,0:T(8,128)(2,1)S(1)}, u32[]{:S(2)}, u32[]{:S(2)}) %collective-permute-start.10) | collective-permute-done | bytes 262176 | tf_op jit(solution)/shard_map/ppermute | solution.py:31
  332.2 21.4 %collective-permute-done.24 = f32[2,16,128,64]{2,3,1,0:T(8,128)S(1)} collective-permute-done((f32[2,16,128,64]{2,3,1,0:T(8,128)S(1)}, f32[2,16,128,64]{2,3,1,0:T(8,128)S(1)}, u32[]{:S(2)}, u32[]{:S(2)}) %collective-permute-start.24) | collective-permute-done | bytes 1048608 | tf_op jit(solution)/shard_map/ppermute | solution.py:21
  358.8 3.4 collective-permute-start.12
  362.2 2.2 fusion.46
  370.8 44.9 %collective-permute-done.12 = bf16[128,1024]{1,0:T(8,128)(2,1)} collective-permute-done((bf16[128,1024]{1,0:T(8,128)(2,1)}, bf16[128,1024]{1,0:T(8,128)(2,1)}, u32[]{:S(2)}, u32[]{:S(2)}) %collective-permute-start.12) | collective-permute-done | bytes 262176 | tf_op jit(solution)/shard_map/ppermute | solution.py:31
  415.7 4.7 %rev.6 = bf16[128,1024]{1,0:T(8,128)(2,1)} reverse(bf16[128,1024]{1,0:T(8,128)(2,1)} %collective-permute-done.12), dimensions={0,1} | reverse | bytes 524288 | tf_op jit(solution)/shard_map/rev | solution.py:115
  420.4 1.8 add_convert_fusion.1
  422.2 2.7 multiply_reduce_fusion.3
  424.9 2.5 fusion.7
  427.4 4.2 bitcast_add_fusion
  431.6 3.3 copy.53
  435.0 1.6 fusion.45
  438.6 2.2 reduce_window_sum.38
  440.8 2.2 reduce_window_sum.39
  443.9 2.0 add_convert_fusion
  446.0 1.5 pad_maximum_fusion
  (198 shorter events, 45.1 us)
Async XLA Ops:
  7.2 172.1 %all-gather.2.cloned.1.call-start = ((), (), s32[]{:S(2)}) async-start(), calls=%async_computation.1 | async-start | bytes 4456448 | tf_op jit(solution)/shard_map/all_gather | solution.py:155
  7.9 439.6 %reduce-scatter.2.cloned.1.call-start = ((), (), s32[]{:S(2)}) async-start(), calls=%async_computation.2 | async-start | bytes 8912896 | tf_op jit(solution)/shard_map/reduce_scatter | solution.py:163
  9.1 164.0 %copy-start.1 = (bf16[2,128,2048]{1,2,0:T(8,128)(2,1)}, bf16[2,128,2048]{1,2,0:T(8,128)(2,1)S(1)}, u32[]{:S(2)}) copy-start(bf16[2,128,2048]{1,2,0:T(8,128)(2,1)S(1)} %copy.46) | copy-start | bytes 3145732
  10.1 28.3 %copy-start.37 = (f32[2,1,16]{2,1,0:T(1,128)}, f32[2,1,16]{2,1,0:T(1,128)S(1)}, u32[]{:S(2)}) copy-start(f32[2,1,16]{2,1,0:T(1,128)S(1)} %slice.37) | copy-start | bytes 388
  10.3 28.1 %copy-start.51 = (f32[2,16]{1,0:T(2,128)}, f32[2,16]{1,0:T(2,128)S(1)}, u32[]{:S(2)}) copy-start(f32[2,16]{1,0:T(2,128)S(1)} %get-tuple-element.387) | copy-start | bytes 388
  11.8 4.6 %collective-permute-start.4 = (f32[2,16,128,64]{2,3,1,0:T(8,128)S(1)}, f32[2,16,128,64]{2,3,1,0:T(8,128)S(1)}, u32[]{:S(2)}, u32[]{:S(2)}) collective-permute-start(f32[2,16,128,64]{2,3,1,0:T(8,128)S(1)} %fusion.35), channel_id=1, source_target_pairs={{0,1},{1,2},{2,3},{3,4},{4,5},{5,6},{6,7},{7,8},{8,9},{9,10},{10,1... | collective-permute-start | bytes 3145736 | tf_op jit(solution)/shard_map/ppermute | solution.py:21
  16.4 22.0 %collective-permute-start.5 = (f32[2,16,128,64]{2,3,1,0:T(8,128)S(1)}, f32[2,16,128,64]{2,3,1,0:T(8,128)S(1)}, u32[]{:S(2)}, u32[]{:S(2)}) collective-permute-start(f32[2,16,128,64]{2,3,1,0:T(8,128)S(1)} %collective-permute-done.4), channel_id=1, source_target_pairs={{0,1},{1,2},{2,3},{3,4},{4,5},{5,6},{6,7},{7,8},{8,9},{9,10},{10,1... | collective-permute-start | bytes 3145736 | tf_op jit(solution)/shard_map/ppermute | solution.py:21
  33.3 5.1 %collective-permute-start = (f32[2,16]{1,0:T(2,128)S(1)}, f32[2,16]{1,0:T(2,128)S(1)}, u32[]{:S(2)}, u32[]{:S(2)}) collective-permute-start(f32[2,16]{1,0:T(2,128)S(1)} %get-tuple-element.387), channel_id=1, source_target_pairs={{0,1},{1,2},{2,3},{3,4},{4,5},{5,6},{6,7},{7,8},{8,9},{9,10},{10,1... | collective-permute-start | bytes 392 | tf_op jit(solution)/shard_map/ppermute | solution.py:21
  38.6 65.1 %copy-start.27 = (bf16[128,1024]{1,0:T(8,128)(2,1)S(1)}, bf16[128,1024]{1,0:T(8,128)(2,1)}, u32[]{:S(2)}) copy-start(bf16[128,1024]{1,0:T(8,128)(2,1)} %param.17) | copy-start | bytes 786436
  38.6 39.3 %collective-permute-start.6 = (f32[2,16,128,64]{2,3,1,0:T(8,128)S(1)}, f32[2,16,128,64]{2,3,1,0:T(8,128)S(1)}, u32[]{:S(2)}, u32[]{:S(2)}) collective-permute-start(f32[2,16,128,64]{2,3,1,0:T(8,128)S(1)} %multiply_add_fusion.7), channel_id=1, source_target_pairs={{0,2},{1,3},{2,4},{3,5},{4,6},{5,7},{6,8},{7,9},{8,10},{9,11},{10,... | collective-permute-start | bytes 3145736 | tf_op jit(solution)/shard_map/ppermute | solution.py:21
  63.3 12.2 %collective-permute-start.1 = (f32[2,16]{1,0:T(2,128)S(1)}, f32[2,16]{1,0:T(2,128)S(1)}, u32[]{:S(2)}, u32[]{:S(2)}) collective-permute-start(f32[2,16]{1,0:T(2,128)S(1)} %collective-permute-done), channel_id=1, source_target_pairs={{0,1},{1,2},{2,3},{3,4},{4,5},{5,6},{6,7},{7,8},{8,9},{9,10},{10,1... | collective-permute-start | bytes 392 | tf_op jit(solution)/shard_map/ppermute | solution.py:21
  78.1 42.4 %collective-permute-start.7 = (f32[2,16,128,64]{2,3,1,0:T(8,128)S(1)}, f32[2,16,128,64]{2,3,1,0:T(8,128)S(1)}, u32[]{:S(2)}, u32[]{:S(2)}) collective-permute-start(f32[2,16,128,64]{2,3,1,0:T(8,128)S(1)} %multiply_add_fusion.6), channel_id=1, source_target_pairs={{0,4},{1,5},{2,6},{3,7},{4,8},{5,9},{6,10},{7,11},{8,12},{9,13},{1... | collective-permute-start | bytes 3145736 | tf_op jit(solution)/shard_map/ppermute | solution.py:21
  100.0 4.9 %collective-permute-start.2 = (f32[2,16]{1,0:T(2,128)S(1)}, f32[2,16]{1,0:T(2,128)S(1)}, u32[]{:S(2)}, u32[]{:S(2)}) collective-permute-start(f32[2,16]{1,0:T(2,128)S(1)} %mul.542), channel_id=1, source_target_pairs={{0,2},{1,3},{2,4},{3,5},{4,6},{5,7},{6,8},{7,9},{8,10},{9,11},{10,... | collective-permute-start | bytes 392 | tf_op jit(solution)/shard_map/ppermute | solution.py:21
  103.7 25.4 %collective-permute-start.13 = (bf16[128,1024]{1,0:T(8,128)(2,1)S(1)}, bf16[128,1024]{1,0:T(8,128)(2,1)S(1)}, u32[]{:S(2)}, u32[]{:S(2)}) collective-permute-start(bf16[128,1024]{1,0:T(8,128)(2,1)S(1)} %copy-done.27), channel_id=1, source_target_pairs={{0,1},{1,0},{2,3},{3,2},{4,5},{5,4},{6,7},{7,6},{8,9},{9,8},{10,11... | collective-permute-start | bytes 786440 | tf_op jit(solution)/shard_map/ppermute | solution.py:31
  120.7 49.1 %collective-permute-start.8 = (f32[2,16,128,64]{2,3,1,0:T(8,128)S(1)}, f32[2,16,128,64]{2,3,1,0:T(8,128)}, u32[]{:S(2)}, u32[]{:S(2)}) collective-permute-start(f32[2,16,128,64]{2,3,1,0:T(8,128)S(1)} %multiply_add_fusion.5), channel_id=1, source_target_pairs={{0,8},{1,9},{2,10},{3,11},{4,12},{5,13},{6,14},{7,15},{16,24},{17,... | collective-permute-start | bytes 3145736 | tf_op jit(solution)/shard_map/ppermute | solution.py:21
  129.1 6.4 %collective-permute-start.14 = (bf16[128,1024]{1,0:T(8,128)(2,1)S(1)}, bf16[128,1024]{1,0:T(8,128)(2,1)S(1)}, u32[]{:S(2)}, u32[]{:S(2)}) collective-permute-start(bf16[128,1024]{1,0:T(8,128)(2,1)S(1)} %collective-permute-done.13), channel_id=1, source_target_pairs={{0,2},{2,0},{1,3},{3,1},{4,6},{6,4},{5,7},{7,5},{8,10},{10,8},{9,1... | collective-permute-start | bytes 786440 | tf_op jit(solution)/shard_map/ppermute | solution.py:31
  135.4 21.3 %collective-permute-start.15 = (bf16[128,1024]{1,0:T(8,128)(2,1)S(1)}, bf16[128,1024]{1,0:T(8,128)(2,1)S(1)}, u32[]{:S(2)}, u32[]{:S(2)}) collective-permute-start(bf16[128,1024]{1,0:T(8,128)(2,1)S(1)} %collective-permute-done.14), channel_id=1, source_target_pairs={{0,4},{4,0},{1,5},{5,1},{2,6},{6,2},{3,7},{7,3},{8,12},{12,8},{9,1... | collective-permute-start | bytes 786440 | tf_op jit(solution)/shard_map/ppermute | solution.py:31
  135.7 176.7 %copy-start.35 = (pred[128,128]{1,0:T(8,128)(4,1)}, pred[128,128]{1,0:T(8,128)(4,1)S(1)}, u32[]{:S(2)}) copy-start(pred[128,128]{1,0:T(8,128)(4,1)S(1)} %iota_compare_fusion) | copy-start | bytes 49156
  135.8 176.7 %copy-start.30 = (f32[2,128,16]{1,2,0:T(8,128)}, f32[2,128,16]{1,2,0:T(8,128)S(1)}, u32[]{:S(2)}) copy-start(f32[2,128,16]{1,2,0:T(8,128)S(1)} %copy.43) | copy-start | bytes 49156
  156.7 10.1 %collective-permute-start.16 = (bf16[128,1024]{1,0:T(8,128)(2,1)S(1)}, bf16[128,1024]{1,0:T(8,128)(2,1)S(1)}, u32[]{:S(2)}, u32[]{:S(2)}) collective-permute-start(bf16[128,1024]{1,0:T(8,128)(2,1)S(1)} %collective-permute-done.15), channel_id=1, source_target_pairs={{0,8},{8,0},{1,9},{9,1},{2,10},{10,2},{3,11},{11,3},{4,12},{12,4},... | collective-permute-start | bytes 786440 | tf_op jit(solution)/shard_map/ppermute | solution.py:31
  159.1 5.7 %collective-permute-start.3 = (f32[2,16]{1,0:T(2,128)S(1)}, f32[2,16]{1,0:T(2,128)S(1)}, u32[]{:S(2)}, u32[]{:S(2)}) collective-permute-start(f32[2,16]{1,0:T(2,128)S(1)} %mul.543), channel_id=1, source_target_pairs={{0,4},{1,5},{2,6},{3,7},{4,8},{5,9},{6,10},{7,11},{8,12},{9,13},{1... | collective-permute-start | bytes 392 | tf_op jit(solution)/shard_map/ppermute | solution.py:21
  163.7 148.8 %copy-start.32 = (f32[2,128,16]{1,2,0:T(8,128)}, f32[2,128,16]{1,2,0:T(8,128)S(1)}, u32[]{:S(2)}) copy-start(f32[2,128,16]{1,2,0:T(8,128)S(1)} %copy.45) | copy-start | bytes 49156
  194.3 7.3 %copy-start.52 = (f32[2,16]{1,0:T(2,128)S(1)}, f32[2,16]{1,0:T(2,128)}, u32[]{:S(2)}) copy-start(f32[2,16]{1,0:T(2,128)} %copy-done.51) | copy-start | bytes 388
  195.8 66.3 %copy-start.54 = (f32[16]{0:T(128)S(1)}, f32[16]{0:T(128)}, u32[]{:S(2)}) copy-start(f32[16]{0:T(128)} %param.14) | copy-start | bytes 196
  195.8 4.6 %collective-permute-start.21 = (f32[2,16,128,64]{2,3,1,0:T(8,128)S(1)}, f32[2,16,128,64]{2,3,1,0:T(8,128)S(1)}, u32[]{:S(2)}, u32[]{:S(2)}) collective-permute-start(f32[2,16,128,64]{2,3,1,0:T(8,128)S(1)} %fusion.31), channel_id=1, source_target_pairs={{1,0},{2,1},{3,2},{4,3},{5,4},{6,5},{7,6},{8,7},{9,8},{10,9},{11,1... | collective-permute-start | bytes 3145736 | tf_op jit(solution)/shard_map/ppermute | solution.py:21
  200.4 15.0 %collective-permute-start.22 = (f32[2,16,128,64]{2,3,1,0:T(8,128)S(1)}, f32[2,16,128,64]{2,3,1,0:T(8,128)S(1)}, u32[]{:S(2)}, u32[]{:S(2)}) collective-permute-start(f32[2,16,128,64]{2,3,1,0:T(8,128)S(1)} %collective-permute-done.21), channel_id=1, source_target_pairs={{1,0},{2,1},{3,2},{4,3},{5,4},{6,5},{7,6},{8,7},{9,8},{10,9},{11,1... | collective-permute-start | bytes 3145736 | tf_op jit(solution)/shard_map/ppermute | solution.py:21
  201.7 13.7 %collective-permute-start.17 = (f32[2,16]{1,0:T(2,128)S(1)}, f32[2,16]{1,0:T(2,128)S(1)}, u32[]{:S(2)}, u32[]{:S(2)}) collective-permute-start(f32[2,16]{1,0:T(2,128)S(1)} %copy-done.52), channel_id=1, source_target_pairs={{1,0},{2,1},{3,2},{4,3},{5,4},{6,5},{7,6},{8,7},{9,8},{10,9},{11,1... | collective-permute-start | bytes 392 | tf_op jit(solution)/shard_map/ppermute | solution.py:21
  215.3 95.0 %copy-start.55 = (bf16[2048,1024]{1,0:T(8,128)(2,1)S(1)}, bf16[2048,1024]{1,0:T(8,128)(2,1)}, u32[]{:S(2)}) copy-start(bf16[2048,1024]{1,0:T(8,128)(2,1)} %all-gather.2.cloned.1.call-done) | copy-start | bytes 12582916
  215.5 94.9 %copy-start.13 = (bf16[2,128,2048]{2,1,0:T(8,128)(2,1)S(1)}, bf16[2,128,2048]{2,1,0:T(8,128)(2,1)}, u32[]{:S(2)}) copy-start(bf16[2,128,2048]{2,1,0:T(8,128)(2,1)} %copy-done.12) | copy-start | bytes 3145732
  215.5 93.2 %collective-permute-start.23 = (f32[2,16,128,64]{2,3,1,0:T(8,128)S(1)}, f32[2,16,128,64]{2,3,1,0:T(8,128)S(1)}, u32[]{:S(2)}, u32[]{:S(2)}) collective-permute-start(f32[2,16,128,64]{2,3,1,0:T(8,128)S(1)} %multiply_add_fusion.3), channel_id=1, source_target_pairs={{2,0},{3,1},{4,2},{5,3},{6,4},{7,5},{8,6},{9,7},{10,8},{11,9},{12,... | collective-permute-start | bytes 3145736 | tf_op jit(solution)/shard_map/ppermute | solution.py:21
  217.1 14.4 %collective-permute-start.18 = (f32[2,16]{1,0:T(2,128)S(1)}, f32[2,16]{1,0:T(2,128)S(1)}, u32[]{:S(2)}, u32[]{:S(2)}) collective-permute-start(f32[2,16]{1,0:T(2,128)S(1)} %collective-permute-done.17), channel_id=1, source_target_pairs={{1,0},{2,1},{3,2},{4,3},{5,4},{6,5},{7,6},{8,7},{9,8},{10,9},{11,1... | collective-permute-start | bytes 392 | tf_op jit(solution)/shard_map/ppermute | solution.py:21
  231.4 29.4 %collective-permute-start.19 = (f32[2,16]{1,0:T(2,128)S(1)}, f32[2,16]{1,0:T(2,128)S(1)}, u32[]{:S(2)}, u32[]{:S(2)}) collective-permute-start(f32[2,16]{1,0:T(2,128)S(1)} %mul.578), channel_id=1, source_target_pairs={{2,0},{3,1},{4,2},{5,3},{6,4},{7,5},{8,6},{9,7},{10,8},{11,9},{12,... | collective-permute-start | bytes 392 | tf_op jit(solution)/shard_map/ppermute | solution.py:21
  260.8 47.3 %collective-permute-start.20 = (f32[2,16]{1,0:T(2,128)S(1)}, f32[2,16]{1,0:T(2,128)S(1)}, u32[]{:S(2)}, u32[]{:S(2)}) collective-permute-start(f32[2,16]{1,0:T(2,128)S(1)} %mul.579), channel_id=1, source_target_pairs={{4,0},{5,1},{6,2},{7,3},{8,4},{9,5},{10,6},{11,7},{12,8},{13,9},{1... | collective-permute-start | bytes 392 | tf_op jit(solution)/shard_map/ppermute | solution.py:21
  308.8 44.7 %collective-permute-start.24 = (f32[2,16,128,64]{2,3,1,0:T(8,128)S(1)}, f32[2,16,128,64]{2,3,1,0:T(8,128)S(1)}, u32[]{:S(2)}, u32[]{:S(2)}) collective-permute-start(f32[2,16,128,64]{2,3,1,0:T(8,128)S(1)} %multiply_add_fusion.2), channel_id=1, source_target_pairs={{4,0},{5,1},{6,2},{7,3},{8,4},{9,5},{10,6},{11,7},{12,8},{13,9},{1... | collective-permute-start | bytes 3145736 | tf_op jit(solution)/shard_map/ppermute | solution.py:21
  311.7 4.9 %collective-permute-start.9 = (bf16[128,1024]{1,0:T(8,128)(2,1)S(1)}, bf16[128,1024]{1,0:T(8,128)(2,1)S(1)}, u32[]{:S(2)}, u32[]{:S(2)}) collective-permute-start(bf16[128,1024]{1,0:T(8,128)(2,1)S(1)} %slice.39), channel_id=1, source_target_pairs={{0,1},{1,0},{2,3},{3,2},{4,5},{5,4},{6,7},{7,6},{8,9},{9,8},{10,11... | collective-permute-start | bytes 786440 | tf_op jit(solution)/shard_map/ppermute | solution.py:31
  312.5 6.5 %copy-start.8 = (f32[2,16,128,128]{3,2,1,0:T(8,128)S(1)}, f32[2,16,128,128]{3,2,1,0:T(8,128)}, u32[]{:S(2)}) copy-start(f32[2,16,128,128]{3,2,1,0:T(8,128)} %fusion.71) | copy-start | bytes 6291460
  312.5 6.5 %copy-start.10 = (f32[2,16,128,128]{3,2,1,0:T(8,128)S(1)}, f32[2,16,128,128]{3,2,1,0:T(8,128)}, u32[]{:S(2)}) copy-start(f32[2,16,128,128]{3,2,1,0:T(8,128)} %copy-done.9) | copy-start | bytes 6291460
  316.6 40.7 %copy-start.26 = (f32[2,128,128]{2,1,0:T(8,128)}, f32[2,128,128]{2,1,0:T(8,128)S(1)}, u32[]{:S(2)}) copy-start(f32[2,128,128]{2,1,0:T(8,128)S(1)} %get-tuple-element.365) | copy-start | bytes 393220
  316.6 14.0 %collective-permute-start.10 = (bf16[128,1024]{1,0:T(8,128)(2,1)S(1)}, bf16[128,1024]{1,0:T(8,128)(2,1)S(1)}, u32[]{:S(2)}, u32[]{:S(2)}) collective-permute-start(bf16[128,1024]{1,0:T(8,128)(2,1)S(1)} %collective-permute-done.9), channel_id=1, source_target_pairs={{0,2},{2,0},{1,3},{3,1},{4,6},{6,4},{5,7},{7,5},{8,10},{10,8},{9,1... | collective-permute-start | bytes 786440 | tf_op jit(solution)/shard_map/ppermute | solution.py:31
  330.7 28.1 %collective-permute-start.11 = (bf16[128,1024]{1,0:T(8,128)(2,1)S(1)}, bf16[128,1024]{1,0:T(8,128)(2,1)}, u32[]{:S(2)}, u32[]{:S(2)}) collective-permute-start(bf16[128,1024]{1,0:T(8,128)(2,1)S(1)} %collective-permute-done.10), channel_id=1, source_target_pairs={{0,4},{4,0},{1,5},{5,1},{2,6},{6,2},{3,7},{7,3},{8,12},{12,8},{9,1... | collective-permute-start | bytes 786440 | tf_op jit(solution)/shard_map/ppermute | solution.py:31
  354.7 67.5 %collective-permute-start.25 = (f32[2,16,128,64]{2,3,1,0:T(8,128)}, f32[2,16,128,64]{2,3,1,0:T(8,128)}, u32[]{:S(2)}, u32[]{:S(2)}) collective-permute-start(f32[2,16,128,64]{2,3,1,0:T(8,128)} %multiply_add_fusion.1), channel_id=1, source_target_pairs={{8,0},{9,1},{10,2},{11,3},{12,4},{13,5},{14,6},{15,7},{24,16},{25,... | collective-permute-start | bytes 3145736 | tf_op jit(solution)/shard_map/ppermute | solution.py:21
  357.3 11.5 %copy-start.42 = (f32[2,128,16]{1,2,0:T(8,128)S(1)}, f32[2,128,16]{1,2,0:T(8,128)}, u32[]{:S(2)}) copy-start(f32[2,128,16]{1,2,0:T(8,128)} %get-tuple-element.364) | copy-start | bytes 49156
  358.8 56.9 %collective-permute-start.12 = (bf16[128,1024]{1,0:T(8,128)(2,1)}, bf16[128,1024]{1,0:T(8,128)(2,1)}, u32[]{:S(2)}, u32[]{:S(2)}) collective-permute-start(bf16[128,1024]{1,0:T(8,128)(2,1)} %collective-permute-done.11), channel_id=1, source_target_pairs={{0,8},{8,0},{1,9},{9,1},{2,10},{10,2},{3,11},{11,3},{4,12},{12,4},... | collective-permute-start | bytes 786440 | tf_op jit(solution)/shard_map/ppermute | solution.py:31
  435.0 8.0 %copy-start.21 = (f32[2,128,16]{2,1,0:T(8,128)S(1)}, f32[2,128,16]{2,1,0:T(8,128)}, u32[]{:S(2)}) copy-start(f32[2,128,16]{2,1,0:T(8,128)} %copy.61) | copy-start | bytes 49156
  436.6 6.4 %copy-start.39 = (f32[2,1,16]{2,1,0:T(1,128)S(1)}, f32[2,1,16]{2,1,0:T(1,128)}, u32[]{:S(2)}) copy-start(f32[2,1,16]{2,1,0:T(1,128)} %copy-done.37) | copy-start | bytes 388
  436.6 6.4 %copy-start.45 = (f32[16]{0:T(128)S(1)}, f32[16]{0:T(128)}, u32[]{:S(2)}) copy-start(f32[16]{0:T(128)} %param.12) | copy-start | bytes 196
  436.6 7.3 %copy-start = (f32[2,128,2048]{2,1,0:T(8,128)S(1)}, f32[2,128,2048]{2,1,0:T(8,128)}, u32[]{:S(2)}) copy-start(f32[2,128,2048]{2,1,0:T(8,128)} %get-tuple-element.374) | copy-start | bytes 6291460
  436.6 7.3 %copy-start.40 = (f32[2048]{0:T(1024)S(1)}, f32[2048]{0:T(1024)}, u32[]{:S(2)}) copy-start(f32[2048]{0:T(1024)} %broadcast_bitcast_fusion) | copy-start | bytes 24580
  (38 other events, 96.7 us)
Sparse Core Ops, SparseCore 0:
  10.2 59.7 all-gather.1
  192.5 156.4 reduce-scatter.1
where the time goes:
time: 460 us; the launch traced here: 455 us
  waiting for transfers between devices  232 us (50%)
  starting transfers between devices  119 us (26%)
  matrix products  40.1 us (9%)
  local copies, waits for them, and re-layouts  25.6 us (6%)
  other arithmetic  22.2 us (5%)
  between operations  15.5 us (3%)
    ppermute x18, waiting for transfers between devices, from_behind(): return lax.ppermute(x, axis, pairs)  147 us
    ppermute x18, starting transfers between devices, from_behind(): return lax.ppermute(x, axis, pairs)  110 us
    ppermute x8, waiting for transfers between devices, from_partner(): return lax.ppermute(block, axis, route)  84.1 us
    dot_general x3, matrix products, block_step(): inside = jnp.einsum('tuh,uhp->thp', mixing, x_part, precision=PRECISE)  12.5 us
  transfers between devices with their start and end apart: 28, of which 19 were waited for; matrix products, arithmetic and copies ran while one was open for 16% of the time, Pallas kernels for 0%

commit v1 on v0

v1 whole, which is shorter than its diff:
```python
import functools

import jax
import jax.numpy as jnp
from jax import lax
from jax.experimental import pallas as pl
from jax.experimental.pallas import tpu as pltpu
from jax.sharding import PartitionSpec as P

D = 1024
HEADS = 16
HEAD_DIM = 128
STATE = 64
INNER = 2048
TOK = 128
LANES = 128
ROWS = 2 * HEADS * STATE
EPSILON = 1e-05
HIGH = lax.Precision.HIGHEST
F32 = jnp.float32
BF16 = jnp.bfloat16
MESH = pl.DeviceIdType.MESH
VMEM_LIMIT = 56 * 2**20


def dot(a, b, ca=1, cb=0, precision=None):
    return lax.dot_general(
        a, b, (((ca,), (cb,)), ((), ())), precision=precision, preferred_element_type=F32
    )


def grids(shape=(TOK, TOK)):
    return lax.broadcasted_iota(jnp.int32, shape, 0), lax.broadcasted_iota(jnp.int32, shape, 1)


def anti_identity():
    row, col = grids()
    return (row + col == TOK - 1).astype(BF16)


def flip_both(block):
    anti = anti_identity()
    turned = dot(anti, block).astype(BF16)
    count = block.shape[1] // TOK
    parts = [
        dot(turned[:, (count - 1 - k) * TOK : (count - k) * TOK], anti).astype(BF16)
        for k in range(count)
    ]
    return jnp.concatenate(parts, axis=1)


def steps(raw, bias, dlog):
    arg = raw + bias
    size = jnp.maximum(arg, 0.0) + jnp.log1p(jnp.exp(-jnp.abs(arg)))
    rate = -jnp.exp(dlog) * size
    row, col = grids()
    lower = (row >= col).astype(F32)
    cum = dot(lower, rate, precision=HIGH)
    return arg, size, rate, cum


def head(h):
    return slice(h * HEAD_DIM, (h + 1) * HEAD_DIM)


def srows(h):
    return slice(h * STATE, (h + 1) * STATE)


def local_state_kernel(x_ref, bc_ref, raw_ref, bias_ref, dlog_ref, st_ref, dec_ref):
    _, size, _, cum = steps(raw_ref[0], bias_ref[...], dlog_ref[...])
    total = cum[TOK - 1 : TOK, :]
    weight = jnp.exp(total - cum) * size
    b = bc_ref[0, :, :STATE]
    for h in range(HEADS):
        xw = (x_ref[0, :, head(h)].astype(F32) * weight[:, h : h + 1]).astype(BF16)
        st_ref[0, srows(h), :] = dot(b, xw, 0, 0).astype(BF16)
    dec_ref[0] = jnp.exp(total)


def mixing(scores, mask, cum, cum_t, size_t, h):
    gap = cum[:, h : h + 1] - cum_t[h : h + 1, :]
    decay = jnp.where(mask, jnp.exp(jnp.minimum(gap, 0.0)), 0.0)
    return decay * size_t[h : h + 1, :]


def middle_kernel(
    main_ref, bc_ref, raw_ref, bias_ref, dlog_ref, skip_ref, gain_ref, w_ref, gm_ref, gmm_ref, e_ref,
    nt_ref, so_ref, gz_ref, gy_ref, de_ref, gyy_ref,
    y_s, gn_s, bi_s, no_s,
):
    strand = pl.program_id(0)

    @pl.when(strand == 0)
    def _():
        bi_s[...] = gm_ref[...]

    @pl.when(strand == 1)
    def _():
        bi_s[...] = flip_both(gmm_ref[...])

    gn_s[...] = dot(bi_s[...], w_ref[...], 1, 1) * gain_ref[...]
    _, size, _, cum = steps(raw_ref[0], bias_ref[...], dlog_ref[...])
    cum_t, size_t = cum.T, size.T
    ecum = jnp.exp(cum)
    b, c = bc_ref[0, :, :STATE], bc_ref[0, :, STATE:]
    scores = dot(c, b, 1, 1)
    row, col = grids()
    mask = row >= col
    squares = jnp.zeros((TOK, LANES), F32)
    crossed = jnp.zeros((TOK, LANES), F32)
    for h in range(HEADS):
        m = (scores * mixing(scores, mask, cum, cum_t, size_t, h)).astype(BF16)
        x = main_ref[0, :, head(h)]
        y = dot(m, x) + ecum[:, h : h + 1] * dot(c, e_ref[0, srows(h), :])
        y = y + skip_ref[0:1, h : h + 1] * x.astype(F32)
        y_s[:, head(h)] = y
        z = main_ref[0, :, INNER + h * HEAD_DIM : INNER + (h + 1) * HEAD_DIM].astype(F32)
        gated = y * (z / (1.0 + jnp.exp(-z)))
        squares += gated * gated
        crossed += gated * gn_s[:, head(h)]
    r = lax.rsqrt(jnp.sum(squares, axis=1, keepdims=True) / INNER + EPSILON)
    factor = r * r * r * (jnp.sum(crossed, axis=1, keepdims=True) / INNER)
    spin = jnp.where(strand == 0, (row == col).astype(F32), (row + col == TOK - 1).astype(F32))
    spin = spin.astype(BF16)
    for h in range(HEADS):
        z = main_ref[0, :, INNER + h * HEAD_DIM : INNER + (h + 1) * HEAD_DIM].astype(F32)
        y = y_s[:, head(h)]
        sig = 1.0 / (1.0 + jnp.exp(-z))
        silu = z * sig
        gated = y * silu
        normed = (gated * r * gain_ref[:, head(h)]).astype(BF16)
        no_s[:, head(h)] = normed
        nt_ref[head(h), :] = dot(normed, spin, 0, 0).astype(BF16)
        dgated = r * gn_s[:, head(h)] - gated * factor
        gz_ref[0, :, head(h)] = (dgated * y * (sig * (1.0 + z * (1.0 - sig)))).astype(BF16)
        gy = (dgated * silu).astype(BF16)
        gy_ref[0, :, head(h)] = gy
        gyf = gy.astype(F32)
        scan_y = y - skip_ref[0:1, h : h + 1] * main_ref[0, :, head(h)].astype(F32)
        gyy_ref[0, :, h : h + 1] = jnp.sum(gyf * scan_y, axis=1, keepdims=True)
        de_ref[0, srows(h), :] = dot(c, (gyf * ecum[:, h : h + 1]).astype(BF16), 0, 0).astype(BF16)
    so_ref[0] = dot(no_s[...], w_ref[...]).astype(BF16)


def last_kernel(
    x_ref, gz_ref, gy_ref, bc_ref, raw_ref, bias_ref, dlog_ref, skip_ref, e_ref, lv_ref, gyy_ref,
    gmain_ref, gstate_ref, gstep_ref,
    xdx_s,
):
    arg, size, _, cum = steps(raw_ref[0], bias_ref[...], dlog_ref[...])
    cum_t, size_t = cum.T, size.T
    ecum = jnp.exp(cum)
    total = cum[TOK - 1 : TOK, :]
    weight = jnp.exp(total - cum) * size
    b, c = bc_ref[0, :, :STATE], bc_ref[0, :, STATE:]
    scores = dot(c, b, 1, 1)
    row, col = grids()
    mask = row >= col
    lane = lax.broadcasted_iota(jnp.int32, (1, LANES), 1)
    gscore = jnp.zeros((TOK, TOK), F32)
    gb = jnp.zeros((TOK, STATE), F32)
    gc = jnp.zeros((TOK, STATE), F32)
    gtotal = jnp.zeros((1, LANES), F32)
    xdx_s[...] = jnp.zeros_like(xdx_s)
    for h in range(HEADS):
        w = mixing(scores, mask, cum, cum_t, size_t, h)
        m = (scores * w).astype(BF16)
        x, gy = x_ref[0, :, head(h)], gy_ref[0, :, head(h)]
        xf, gyf = x.astype(F32), gy.astype(F32)
        lv, e = lv_ref[0, srows(h), :], e_ref[0, srows(h), :]
        gscore += dot(gy, x, 1, 1) * w
        wcol = weight[:, h : h + 1]
        through = wcol * dot(b, lv)
        dx = dot(m, gy, 0, 0) + through
        gmain_ref[0, :, head(h)] = (dx + skip_ref[0:1, h : h + 1] * gyf).astype(BF16)
        xdx_s[:, h : h + 1] = jnp.sum(xf * dx, axis=1, keepdims=True)
        gc += dot((gyf * ecum[:, h : h + 1]).astype(BF16), e, 1, 1)
        gb += dot((xf * wcol).astype(BF16), lv, 1, 1)
        held = jnp.sum(xf * through, axis=0, keepdims=True)
        kept = jnp.sum(e.astype(F32) * lv.astype(F32), axis=0, keepdims=True)
        both = jnp.sum(held + jnp.exp(total[:, h : h + 1]) * kept, axis=1, keepdims=True)
        gtotal += jnp.where(lane == h, both, 0.0)
    gs = gscore.astype(BF16)
    gstate_ref[0, :, :STATE] = gb + dot(gs, c, 0, 0)
    gstate_ref[0, :, STATE:] = gc + dot(gs, b)
    gmain_ref[0, :, INNER:] = gz_ref[0]
    real = lane < HEADS
    gcum = jnp.where(real, gyy_ref[0], 0.0) - xdx_s[...]
    upper = (row <= col).astype(F32)
    grate = dot(upper, gcum, precision=HIGH) + gtotal
    gsize = xdx_s[...] / size - jnp.exp(dlog_ref[...]) * grate
    gstep_ref[0] = gsize / (1.0 + jnp.exp(-arg))


def weight_kernel(n, nt_ref, gm_ref, so_ref, som_ref, gw_ref, mixed_ref):
    plain = jnp.zeros(gw_ref.shape, F32)
    turned = jnp.zeros(gw_ref.shape, F32)

    def body(i, held):
        plain, turned = held
        near = gm_ref[pl.ds(pl.multiple_of(i * TOK, TOK), TOK), :]
        far = gm_ref[pl.ds(pl.multiple_of((n - 1 - i) * TOK, TOK), TOK), :]
        return plain + dot(nt_ref[i, :, :TOK], near), turned + dot(nt_ref[i, :, TOK:], far)

    plain, turned = lax.fori_loop(0, n, body, (plain, turned))
    row, col = grids()
    anti = (row + col == TOK - 1).astype(F32)
    count = D // TOK
    for k in range(count):
        back = turned[:, (count - 1 - k) * TOK : (count - k) * TOK]
        gw_ref[:, k * TOK : (k + 1) * TOK] = plain[:, k * TOK : (k + 1) * TOK] + dot(
            back, anti, precision=HIGH
        )
    mixed_ref[...] = (so_ref[...].astype(F32) + flip_both(som_ref[...]).astype(F32)).astype(BF16)


def exchange_kernel(n, backward, *refs):
    if backward:
        (st_ref, dec_ref, block_ref, nt_ref, out_ref, gotblock_ref, gotnt_ref, inbox, outbox) = refs[:9]
        sems = refs[9:]
        st_send, st_recv, out_send, out_recv, block_send, block_recv, nt_send, nt_recv = sems
        decbox = dec_ref
    else:
        (st_ref, dec_ref, block_ref, out_ref, gotblock_ref, decbox, inbox, outbox) = refs[:8]
        sems = refs[8:]
        st_send, st_recv, out_send, out_recv, block_send, block_recv, dec_send, dec_recv = sems
    me = lax.axis_index("seq")
    share = ROWS // n
    inner = INNER // n
    barrier = pltpu.get_barrier_semaphore()

    def greet(k, _):
        pl.semaphore_signal(
            barrier, inc=1, device_id={"seq": lax.rem(me + k, n)}, device_id_type=MESH
        )
        return 0

    lax.fori_loop(1, n, greet, 0)
    pl.semaphore_wait(barrier, n - 1)

    def rows_of(i, size):
        return pl.ds(pl.multiple_of(i * size, size), size)

    def st_copy(to, slot):
        return pltpu.make_async_remote_copy(
            src_ref=st_ref.at[rows_of(to, share), :], dst_ref=inbox.at[slot],
            send_sem=st_send.at[to], recv_sem=st_recv.at[slot],
            device_id={"seq": to}, device_id_type=MESH,
        )

    def dec_copy(to, slot):
        return pltpu.make_async_remote_copy(
            src_ref=dec_ref.at[to], dst_ref=decbox.at[slot],
            send_sem=dec_send.at[to], recv_sem=dec_recv.at[slot],
            device_id={"seq": to}, device_id_type=MESH,
        )

    def nt_copy(to, slot):
        return pltpu.make_async_remote_copy(
            src_ref=nt_ref.at[rows_of(to, inner), :], dst_ref=gotnt_ref.at[slot],
            send_sem=nt_send.at[to], recv_sem=nt_recv.at[slot],
            device_id={"seq": to}, device_id_type=MESH,
        )

    def out_copy(to, slot):
        return pltpu.make_async_remote_copy(
            src_ref=outbox.at[to], dst_ref=out_ref.at[rows_of(slot, share), :],
            send_sem=out_send.at[to], recv_sem=out_recv.at[slot],
            device_id={"seq": to}, device_id_type=MESH,
        )

    def start_st(k, _):
        to = lax.rem(me + k, n)
        if not backward:
            dec_copy(to, me).start()
        st_copy(to, me).start()
        return 0

    lax.fori_loop(1, n, start_st, 0)
    block_copy = pltpu.make_async_remote_copy(
        src_ref=block_ref, dst_ref=gotblock_ref, send_sem=block_send, recv_sem=block_recv,
        device_id={"seq": n - 1 - me}, device_id_type=MESH,
    )
    block_copy.start()
    if backward:
        lax.fori_loop(1, n, lambda k, _: (nt_copy(lax.rem(me + k, n), me).start(), 0)[1], 0)
        gotnt_ref[me] = nt_ref[rows_of(me, inner), :]
    else:
        decbox[me] = dec_ref[me]
    inbox[me] = st_ref[rows_of(me, share), :]

    def arrive(k, _):
        other = lax.rem(me + k, n)
        if not backward:
            dec_copy(other, other).wait_recv()
        st_copy(other, other).wait_recv()
        return 0

    lax.fori_loop(1, n, arrive, 0)

    groups = max(1, share // STATE)
    size = share // groups

    def scan(k, held):
        i = n - 1 - k if backward else k
        outbox[i] = held.astype(BF16)

        @pl.when(i != me)
        def _():
            out_copy(i, me).start()

        grown = [
            held[g * size : (g + 1) * size] * decbox[i, g : g + 1, :] for g in range(groups)
        ]
        grown = grown[0] if groups == 1 else jnp.concatenate(grown, axis=0)
        return grown + inbox[i].astype(F32)

    lax.fori_loop(0, n, scan, jnp.zeros((share, LANES), F32))
    out_ref[rows_of(me, share), :] = outbox[me]

    def finish(k, _):
        other = lax.rem(me + k, n)
        out_copy(other, other).wait_recv()
        out_copy(other, me).wait_send()
        st_copy(other, me).wait_send()
        if backward:
            nt_copy(other, other).wait_recv()
            nt_copy(other, me).wait_send()
        else:
            dec_copy(other, me).wait_send()
        return 0

    lax.fori_loop(1, n, finish, 0)
    block_copy.wait()


def exchange(n, backward, *operands):
    share = ROWS // n
    outs = [jax.ShapeDtypeStruct((ROWS, LANES), BF16), jax.ShapeDtypeStruct((TOK, D), BF16)]
    if backward:
        outs.append(jax.ShapeDtypeStruct((n, INNER // n, 2 * TOK), BF16))
    else:
        outs.append(jax.ShapeDtypeStruct((n, 8, LANES), F32))
    dma = pltpu.SemaphoreType.DMA
    vmem = pl.BlockSpec(memory_space=pltpu.VMEM)
    return pl.pallas_call(
        functools.partial(exchange_kernel, n, backward),
        out_shape=outs,
        in_specs=[vmem] * len(operands),
        out_specs=[vmem] * 3,
        scratch_shapes=[
            pltpu.VMEM((n, share, LANES), BF16),
            pltpu.VMEM((n, share, LANES), BF16),
            dma((n,)), dma((n,)), dma((n,)), dma((n,)), dma, dma, dma((n,)), dma((n,)),
        ],
        compiler_params=pltpu.CompilerParams(
            collective_id=1 if backward else 0, has_side_effects=True, vmem_limit_bytes=VMEM_LIMIT
        ),
    )(*operands)


def strand_block(*shape):
    return pl.BlockSpec((1,) + shape, lambda s: (s,) + (0,) * len(shape))


def fixed_block(*shape):
    return pl.BlockSpec(shape, lambda s: (0,) * len(shape))


def out_of(*shape, dtype=BF16):
    return jax.ShapeDtypeStruct(shape, dtype)


PARAMS = pltpu.CompilerParams(vmem_limit_bytes=VMEM_LIMIT)


def cost(flops, count):
    return pl.CostEstimate(flops=flops, bytes_accessed=count, transcendentals=0)


def per_device(
    proj_main, proj_state, step_raw, step_bias, decay_log, skip_scale, norm_gain, out_weight, grad_mixed
):
    n = lax.axis_size("seq")
    share = ROWS // n
    spare = LANES - HEADS
    raw = jnp.pad(step_raw, ((0, 0), (0, 0), (0, spare)))
    bias, dlog, skip = (
        jnp.pad(v, (0, spare)).reshape(1, LANES) for v in (step_bias, decay_log, skip_scale)
    )
    gain = norm_gain.reshape(1, INNER)
    whole_weight = lax.all_gather(out_weight, "seq", axis=0, tiled=True)
    whole_grad = lax.all_gather(grad_mixed, "seq", axis=0, tiled=True)

    main_x = pl.BlockSpec((1, TOK, INNER), lambda s: (s, 0, 0))
    row = fixed_block(1, LANES)
    state_rows = HEADS * STATE
    st, dec = pl.pallas_call(
        local_state_kernel,
        grid=(2,),
        in_specs=[main_x, strand_block(TOK, 2 * STATE), strand_block(TOK, LANES), row, row],
        out_specs=[strand_block(state_rows, LANES), strand_block(1, LANES)],
        out_shape=[out_of(2, state_rows, LANES), out_of(2, 1, LANES, dtype=F32)],
        compiler_params=PARAMS,
    )(proj_main, proj_state, raw, bias, dlog)
    decays = dec[:, 0, :HEADS].reshape(2 * HEADS)
    table = [[min(j * share // STATE + k, 2 * HEADS - 1) for k in range(8)] for j in range(n)]
    decs = jnp.broadcast_to(decays[jnp.array(table)][:, :, None], (n, 8, LANES))
    entering, grad_far, decbox = exchange(n, False, st.reshape(ROWS, LANES), decs, grad_mixed)
    entering = entering.reshape(2, state_rows, LANES)

    nt, so, gz, gy, de, gyy = pl.pallas_call(
        middle_kernel,
        grid=(2,),
        in_specs=[
            strand_block(TOK, 2 * INNER), strand_block(TOK, 2 * STATE), strand_block(TOK, LANES),
            row, row, row, fixed_block(1, INNER), fixed_block(INNER, D), fixed_block(TOK, D),
            fixed_block(TOK, D), strand_block(state_rows, LANES),
        ],
        out_specs=[
            pl.BlockSpec((INNER, TOK), lambda s: (0, s)), strand_block(TOK, D),
            strand_block(TOK, INNER), strand_block(TOK, INNER), strand_block(state_rows, LANES),
            strand_block(TOK, LANES),
        ],
        out_shape=[
            out_of(INNER, 2 * TOK), out_of(2, TOK, D), out_of(2, TOK, INNER), out_of(2, TOK, INNER),
            out_of(2, state_rows, LANES), out_of(2, TOK, LANES, dtype=F32),
        ],
        scratch_shapes=[
            pltpu.VMEM((TOK, INNER), F32), pltpu.VMEM((TOK, INNER), F32),
            pltpu.VMEM((TOK, D), BF16), pltpu.VMEM((TOK, INNER), BF16),
        ],
        compiler_params=PARAMS,
    )(proj_main, proj_state, raw, bias, dlog, skip, gain, whole_weight, grad_mixed, grad_far, entering)

    leaving, so_far, all_nt = exchange(n, True, de.reshape(ROWS, LANES), decbox, so[1], nt)
    leaving = leaving.reshape(2, state_rows, LANES)

    grad_main, grad_state, grad_step = pl.pallas_call(
        last_kernel,
        grid=(2,),
        in_specs=[
            main_x, strand_block(TOK, INNER), strand_block(TOK, INNER), strand_block(TOK, 2 * STATE),
            strand_block(TOK, LANES), row, row, row, strand_block(state_rows, LANES),
            strand_block(state_rows, LANES), strand_block(TOK, LANES),
        ],
        out_specs=[strand_block(TOK, 2 * INNER), strand_block(TOK, 2 * STATE), strand_block(TOK, LANES)],
        out_shape=[
            out_of(2, TOK, 2 * INNER), out_of(2, TOK, 2 * STATE, dtype=F32), out_of(2, TOK, LANES, dtype=F32),
        ],
        scratch_shapes=[pltpu.VMEM((TOK, LANES), F32)],
        compiler_params=PARAMS,
    )(proj_main, gz, gy, proj_state, raw, bias, dlog, skip, entering, leaving, gyy)

    vmem = pl.BlockSpec(memory_space=pltpu.VMEM)
    grad_weight, mixed_out = pl.pallas_call(
        functools.partial(weight_kernel, n),
        in_specs=[vmem] * 4,
        out_specs=[vmem] * 2,
        out_shape=[out_of(INNER // n, D, dtype=F32), out_of(TOK, D)],
        compiler_params=PARAMS,
    )(all_nt, whole_grad, so[0], so_far)
    return mixed_out, grad_main, grad_state, grad_step[:, :, :HEADS], grad_weight


def solution(mesh):
    placed = (
        P(None, ("parts", "seq"), None), P(None, ("parts", "seq"), None),
        P(None, ("parts", "seq"), None), P(), P(), P(), P(), P("seq", None),
        P(("parts", "seq"), None),
    )
    return jax.shard_map(
        per_device,
        mesh=mesh,
        in_specs=placed,
        out_specs=(
            P(("parts", "seq"), None), P(None, ("parts", "seq"), None),
            P(None, ("parts", "seq"), None), P(None, ("parts", "seq"), None),
            P(("parts", "seq"), None),
        ),
        check_vma=False,
    )
```

time: 460 us -> 218 us (0.47); the launches traced: 455 us -> 218 us
  waiting for transfers between devices: 232 us -> 9.36 us
  Pallas kernels: 0 us -> 184 us
  starting transfers between devices: 119 us -> 0.08 us
  matrix products: 40.1 us -> 0 us
  other arithmetic: 22.2 us -> 0.66 us
  local copies, waits for them, and re-layouts: 25.6 us -> 9.5 us
    ppermute x26 -> x0, waiting for transfers between devices: 231 us -> none  [the longest x18 147 us: from_behind(): return lax.ppermute(x, axis, pairs)]
    pallas_call x0 -> x6, Pallas kernels: none -> 184 us  [the longest x2 143 us: exchange(): pl.pallas_call(functools.partial(exchange_kernel, n, backward), out_shape...]
    ppermute x26 -> x0, starting transfers between devices: 119 us -> none  [the longest x18 110 us: from_behind(): return lax.ppermute(x, axis, pairs)]
    dot_general x17 -> x0, matrix products: 40.1 us -> none  [the longest x3 12.5 us: block_step(): inside = jnp.einsum('tuh,uhp->thp', mixing, x_part, precision=PRECISE)]
    all_gather x1, waiting for transfers between devices: 0.02 us -> 7.98 us  [per_device(): whole_weight = lax.all_gather(out_weight, 'seq', axis=0, tiled=True)]
    rev x2 -> x0, local copies, waits for them, and re-layouts: 7.62 us -> none  [mirror(): return (moved_first[::-1, ::-1], moved_second[::-1, ::-1])]
    another operation x4 -> x0, other arithmetic: 6.68 us -> none  [the longest x2 2.41 us: block_step(): cumulative = jnp.cumsum(rate_part, axis=0)]
    reduce_sum x6 -> x0, local copies, waits for them, and re-layouts: 5.3 us -> none  [the longest x2 2.94 us: block_step(): gaps_log = cumulative[:, None, :] - cumulative[None, :, :]]
  transfers between devices with their start and end apart: 28 -> 2, of which waited for: 19 -> 1; matrix products, arithmetic and copies ran while one was open for 16% -> 5% of each run, Pallas kernels for 0% -> 80%
where the time goes in v1:
time: 218 us
  Pallas kernels  184 us (84%)
  between operations  14.1 us (6%)
  local copies, waits for them, and re-layouts  9.5 us (4%)
  waiting for transfers between devices  9.36 us (4%)
    pallas_call x2, Pallas kernels, exchange(): pl.pallas_call(functools.partial(exchange_kernel, n, backward), out_shape...  143 us
    pallas_call x1, Pallas kernels, per_device(): pl.pallas_call(middle_kernel, grid=(2,), in_specs=[strand_block(TOK, 2 *...  14.5 us
    pallas_call x1, Pallas kernels, per_device(): pl.pallas_call(last_kernel, grid=(2,), in_specs=[main_x, strand_block(TOK...  12.2 us
    pallas_call x1, Pallas kernels, per_device(): pl.pallas_call(functools.partial(weight_kernel, n), in_specs=[vmem] * 4,...  10.6 us
    all_gather x1, waiting for transfers between devices, per_device(): whole_weight = lax.all_gather(out_weight, 'seq', axis=0, tiled=True)  7.98 us
  transfers between devices with their start and end apart: 2, of which 1 were waited for; matrix products, arithmetic and copies ran while one was open for 5% of the time, Pallas kernels for 80%

profile of v1, /device:TPU:0, one launch (start us, length us, event | category | flops | bytes accessed | tf_op | source)
XLA Modules:
  0.0 217.8 jit_solution(739415331027553212)
XLA Ops:
  7.2 0.0 all-gather.3.cloned.1.call-start
  7.2 0.7 all-gather.3.cloned.1.call-update
  7.9 0.0 all-gather.5.cloned.1.call-start
  7.9 0.7 all-gather.5.cloned.1.call-update
  8.6 0.8 copy.17
  9.5 0.7 pad.14.raw_ref
  10.1 1.2 pad_bitcast_fusion.1
  11.4 3.5 %shard_map.137 = (bf16[2,1024,128]{2,1,0:T(8,128)(2,1)}, f32[2,1,128]{2,1,0:T(1,128)}) custom-call(bf16[2,128,4096]{2,1,0:T(8,128)(2,1)} %x_ref.3, bf16[2,128,128]{2,1,0:T(8,128)(2,1)} %bc_ref.5, f32[2,128,128]{2,1,0:T(8,128)} %pad.14.raw_ref, f32[1,128]{1,0:T(1,128)} %get-tuple-element.56.bias_ref, f32[1,128]{1,0:T(1,128)} %get-tuple-element.55.dlog_ref), custom_call_target="tpu_custom_call" | custom-call | tf_op jit(solution)/shard_map/pallas_call | solution.py:399
  14.9 0.7 slice_reduce_fusion
  15.6 0.1 reshape_squeeze.3
  15.7 0.7 pad_clamp_fusion
  16.3 0.0 copy-start
  16.3 1.2 gather_fusion
  17.6 0.1 reshape.44
  17.6 0.7 broadcast_in_dim.10.refs_1_
  18.4 60.4 %shard_map.138 = (bf16[2048,128]{1,0:T(8,128)(2,1)}, bf16[128,1024]{1,0:T(8,128)(2,1)}, f32[16,8,128]{2,1,0:T(8,128)}) custom-call(bf16[2048,128]{1,0:T(8,128)(2,1)} %bitcast.19, f32[16,8,128]{2,1,0:T(8,128)} %broadcast_in_dim.10.refs_1_, bf16[128,1024]{1,0:T(8,128)(2,1)} %gm_ref.1), custom_call_target="tpu_custom_call" | custom-call | tf_op jit(solution)/shard_map/pallas_call | solution.py:347
  78.8 0.0 copy-done
  78.8 0.5 pad_bitcast_fusion.skip_ref
  79.3 8.0 %all-gather.3.cloned.1.call-done.w_ref = bf16[2048,1024]{1,0:T(8,128)(2,1)} async-done(((bf16[128,1024]{1,0:T(8,128)(2,1)}), bf16[2048,1024]{1,0:T(8,128)(2,1)}) %all-gather.3.cloned.1.call-update) | async-done | bytes 4194320 | tf_op jit(solution)/shard_map/all_gather | solution.py:393
  87.3 14.5 %shard_map.139 = (bf16[2048,256]{1,0:T(8,128)(2,1)}, bf16[2,128,1024]{2,1,0:T(8,128)(2,1)}, bf16[2,128,2048]{2,1,0:T(8,128)(2,1)}, bf16[2,128,2048]{2,1,0:T(8,12...) custom-call(bf16[2,128,4096]{2,1,0:T(8,128)(2,1)} %x_ref.3, bf16[2,128,128]{2,1,0:T(8,128)(2,1)} %bc_ref.5, ...), custom_call_target="tpu_custom_call" | custom-call | tf_op jit(solution)/shard_map/pallas_call | solution.py:413
  101.8 1.9 slice_bitcast_fusion
  103.7 82.9 %shard_map.140 = (bf16[2048,128]{1,0:T(8,128)(2,1)}, bf16[128,1024]{1,0:T(8,128)(2,1)}, bf16[16,128,256]{2,1,0:T(8,128)(2,1)}) custom-call(bf16[2048,128]{1,0:T(8,128)(2,1)} %bitcast.20, f32[16,8,128]{2,1,0:T(8,128)} %get-tuple-element.29.refs_1_, bf16[128,1024]{1,0:T(8,128)(2,1)} %get-tuple-element.54.refs_2_, bf16[2048,256]{1,0:T(8,128)(2,1)} %get-tuple-element.31.refs_3_), custom_call_target="tpu_custom_call" | custom-call | tf_op jit(solution)/shard_map/pallas_call | solution.py:347
  186.6 12.2 %shard_map.142 = (bf16[2,128,4096]{2,1,0:T(8,128)(2,1)}, f32[2,128,128]{2,1,0:T(8,128)}, f32[2,128,128]{2,1,0:T(8,128)}) custom-call(bf16[2,128,4096]{2,1,0:T(8,128)(2,1)} %x_ref.3, bf16[2,128,2048]{2,1,0:T(8,128)(2,1)} %get-tuple-element.35.gz_ref, bf16[2,128,2048]{2,1,0:T(8,128)(2,1)} %get-tuple-element.36.gy_ref, bf16[2,128,128]{2,1,0:T(8,128)(2,1)} %bc_ref.5, ...), custom_call_target="tpu_custom_call" | custom-call | tf_op jit(solution)/shard_map/pallas_call | solution.py:440
  198.8 1.6 copy.18
  200.4 0.0 all-gather.5.cloned.1.call-done.gm_ref
  200.4 10.6 %shard_map.141 = (f32[128,1024]{1,0:T(8,128)}, bf16[128,1024]{1,0:T(8,128)(2,1)}) custom-call(bf16[16,128,256]{2,1,0:T(8,128)(2,1)} %get-tuple-element.32.nt_ref, bf16[2048,1024]{1,0:T(8,128)(2,1)} %all-gather.5.cloned.1.call-done.gm_ref, bf16[128,1024]{1,0:T(8,128)(2,1)} %get-tuple-element.53.so_ref, bf16[128,1024]{1,0:T(8,128)(2,1)} %get-tuple-element.33.som_ref), custom_call_target="tpu_custom_call" | custom-call | tf_op jit(solution)/shard_map/pallas_call | solution.py:457
Async XLA Ops:
  7.2 80.1 %all-gather.3.cloned.1.call-start = ((), (), s32[]{:S(2)}) async-start(), calls=%async_computation | async-start | bytes 4456448 | tf_op jit(solution)/shard_map/all_gather | solution.py:393
  7.9 192.5 %all-gather.5.cloned.1.call-start = ((), (), s32[]{:S(2)}) async-start(), calls=%async_computation.1 | async-start | bytes 4456448 | tf_op jit(solution)/shard_map/all_gather | solution.py:394
  16.3 62.5 %copy-start = (f32[16]{0:T(128)S(1)}, f32[16]{0:T(128)}, u32[]{:S(2)}) copy-start(f32[16]{0:T(128)} %param.15) | copy-start | bytes 196
Sparse Core Ops, SparseCore 0:
  10.2 77.0 all-gather.2
  89.4 79.8 all-gather.4

commit v2 on v1

--- a/solution.py
+++ b/solution.py
@@ -217,17 +217,23 @@
 
 def exchange_kernel(n, backward, *refs):
     if backward:
-        (st_ref, dec_ref, block_ref, nt_ref, out_ref, gotblock_ref, gotnt_ref, inbox, outbox) = refs[:9]
-        sems = refs[9:]
-        st_send, st_recv, out_send, out_recv, block_send, block_recv, nt_send, nt_recv = sems
-        decbox = dec_ref
+        (st_ref, dec_ref, block_ref, matedec, decbox, nt_ref, out_ref, gotblock_ref, gotnt_ref) = refs[:9]
+        rest = refs[9:]
     else:
-        (st_ref, dec_ref, block_ref, out_ref, gotblock_ref, decbox, inbox, outbox) = refs[:8]
-        sems = refs[8:]
-        st_send, st_recv, out_send, out_recv, block_send, block_recv, dec_send, dec_recv = sems
+        (st_ref, dec_ref, block_ref, w_ref, out_ref, gotblock_ref, matedec, decbox, wall_ref) = refs[:9]
+        rest = refs[9:]
+    (mate, comb, inbox, outbox, fbox, other, decout), sems = rest[:7], rest[7:]
+    (mate_send, mate_recv, in_send, in_recv, f_send, f_recv, last_send, last_recv, block_send, block_recv) = sems[:10]
+    extra = sems[10:]
     me = lax.axis_index("seq")
-    share = ROWS // n
+    chips = n // 2
+    chip, core = me // 2, lax.rem(me, 2)
+    partner = me + 1 - 2 * core
+    half = ROWS // 2
+    share = half // chips
     inner = INNER // n
+    groups = max(1, share // STATE)
+    size = share // groups
     barrier = pltpu.get_barrier_semaphore()
 
     def greet(k, _):
@@ -239,76 +245,143 @@
     lax.fori_loop(1, n, greet, 0)
     pl.semaphore_wait(barrier, n - 1)
 
-    def rows_of(i, size):
-        return pl.ds(pl.multiple_of(i * size, size), size)
-
-    def st_copy(to, slot):
+    def rows_of(i, count):
+        return pl.ds(pl.multiple_of(i * count, count), count)
+
+    def remote(src, dst, send, recv, to):
         return pltpu.make_async_remote_copy(
-            src_ref=st_ref.at[rows_of(to, share), :], dst_ref=inbox.at[slot],
-            send_sem=st_send.at[to], recv_sem=st_recv.at[slot],
+            src_ref=src, dst_ref=dst, send_sem=send, recv_sem=recv,
             device_id={"seq": to}, device_id_type=MESH,
         )
 
+    to_mate = remote(st_ref.at[rows_of(1 - core, half), :], mate, mate_send.at[0], mate_recv.at[0], partner)
+    to_mate.start()
+    dec_mate = None
+    if not backward:
+        dec_mate = remote(dec_ref.at[rows_of(1 - core, HEADS), :], matedec, mate_send.at[1], mate_recv.at[1], partner)
+        dec_mate.start()
+
+    def in_copy(to, slot):
+        return remote(
+            comb.at[rows_of(to, share), :], inbox.at[slot], in_send.at[to], in_recv.at[slot], 2 * to + core
+        )
+
     def dec_copy(to, slot):
-        return pltpu.make_async_remote_copy(
-            src_ref=dec_ref.at[to], dst_ref=decbox.at[slot],
-            send_sem=dec_send.at[to], recv_sem=dec_recv.at[slot],
-            device_id={"seq": to}, device_id_type=MESH,
+        return remote(decout.at[to], decbox.at[slot], extra[0].at[to], extra[1].at[slot], 2 * to + core)
+
+    def f_copy(to, slot):
+        return remote(
+            outbox.at[to], fbox.at[rows_of(slot, share), :], f_send.at[to], f_recv.at[slot], 2 * to + core
         )
 
     def nt_copy(to, slot):
-        return pltpu.make_async_remote_copy(
-            src_ref=nt_ref.at[rows_of(to, inner), :], dst_ref=gotnt_ref.at[slot],
-            send_sem=nt_send.at[to], recv_sem=nt_recv.at[slot],
-            device_id={"seq": to}, device_id_type=MESH,
+        return remote(
+            nt_ref.at[rows_of(to, inner), :], gotnt_ref.at[slot], extra[0].at[to], extra[1].at[slot], to
         )
 
-    def out_copy(to, slot):
-        return pltpu.make_async_remote_copy(
-            src_ref=outbox.at[to], dst_ref=out_ref.at[rows_of(slot, share), :],
-            send_sem=out_send.at[to], recv_sem=out_recv.at[slot],
-            device_id={"seq": to}, device_id_type=MESH,
-        )
-
-    def start_st(k, _):
-        to = lax.rem(me + k, n)
+    block_copy = remote(block_ref, gotblock_ref, block_send, block_recv, n - 1 - me)
+
+    if not backward:
+        w_recv, cw_send, ccw_send, pair_send = extra[2:]
+        place = jnp.where(lax.rem(chip, 2) == 0, chip // 2, chips - 1 - chip // 2)
+
+        def at(offset):
+            pos = lax.rem(place + offset + 2 * chips, chips)
+            return jnp.where(pos < chips // 2, 2 * pos, 2 * (chips - 1 - pos) + 1)
+
+        def w_copy(block, sems_, to):
+            return remote(wall_ref.at[block], wall_ref.at[block], sems_.at[block], w_recv.at[block], to)
+
+        right, left = 2 * at(1) + core, 2 * at(-1) + core
+        cw_steps = chips // 2
+        ccw_steps = chips - 1 - cw_steps
+        sent = []
+
+        def launch(copy):
+            copy.start()
+            sent.append(copy)
+
+        def ring(step):
+            if step < cw_steps:
+                block = 2 * at(-step) + core
+                if step > 0:
+                    w_copy(block, cw_send, right).wait_recv()
+                launch(w_copy(block, cw_send, right))
+                if step > 0:
+                    launch(w_copy(block, pair_send, partner))
+            if step < ccw_steps:
+                block = 2 * at(step) + core
+                if step > 0:
+                    w_copy(block, ccw_send, left).wait_recv()
+                launch(w_copy(block, ccw_send, left))
+                launch(w_copy(block, pair_send, partner))
+            if step == cw_steps:
+                block = 2 * at(-step) + core
+                w_copy(block, cw_send, right).wait_recv()
+                launch(w_copy(block, pair_send, partner))
+            if step == ccw_steps:
+                block = 2 * at(step) + core
+                w_copy(block, ccw_send, left).wait_recv()
+                launch(w_copy(block, pair_send, partner))
+
+        wall_ref[me] = w_ref[...]
+        ring(0)
+
+    def scaled(dec, rows, h):
+        return dec[h : h + 1, :] * rows.astype(F32)
+
+    near_is_me = core == (1 if backward else 0)
+    to_mate.wait_recv()
+    if not backward:
+        dec_mate.wait_recv()
+    mydec = dec_ref[rows_of(core, HEADS), :]
+    itsdec = matedec[...]
+    neardec = jnp.where(near_is_me, mydec, itsdec)
+    fardec = jnp.where(near_is_me, itsdec, mydec)
+    for h in range(HEADS):
+        mine = st_ref[pl.ds(pl.multiple_of(core * half + h * STATE, STATE), STATE), :]
+        its = mate[srows(h), :]
+        near = jnp.where(near_is_me, mine.astype(F32), its.astype(F32))
+        far = jnp.where(near_is_me, its.astype(F32), mine.astype(F32))
+        comb[srows(h), :] = (scaled(fardec, near, h) + far).astype(BF16)
+    if not backward:
+        both = neardec * fardec
+        for j in range(chips):
+            first = j * share // STATE
+            decout[j, :groups, :] = both[first : first + groups, :]
+
+    def start_in(k, _):
+        to = lax.rem(chip + k, chips)
         if not backward:
-            dec_copy(to, me).start()
-        st_copy(to, me).start()
+            dec_copy(to, chip).start()
+        in_copy(to, chip).start()
         return 0
 
-    lax.fori_loop(1, n, start_st, 0)
-    block_copy = pltpu.make_async_remote_copy(
-        src_ref=block_ref, dst_ref=gotblock_ref, send_sem=block_send, recv_sem=block_recv,
-        device_id={"seq": n - 1 - me}, device_id_type=MESH,
-    )
+    lax.fori_loop(1, chips, start_in, 0)
     block_copy.start()
+    inbox[chip] = comb[rows_of(chip, share), :]
     if backward:
         lax.fori_loop(1, n, lambda k, _: (nt_copy(lax.rem(me + k, n), me).start(), 0)[1], 0)
         gotnt_ref[me] = nt_ref[rows_of(me, inner), :]
     else:
-        decbox[me] = dec_ref[me]
-    inbox[me] = st_ref[rows_of(me, share), :]
+        decbox[chip] = decout[chip]
 
     def arrive(k, _):
-        other = lax.rem(me + k, n)
+        peer = lax.rem(chip + k, chips)
         if not backward:
-            dec_copy(other, other).wait_recv()
-        st_copy(other, other).wait_recv()
+            dec_copy(peer, peer).wait_recv()
+        in_copy(peer, peer).wait_recv()
         return 0
 
-    lax.fori_loop(1, n, arrive, 0)
-
-    groups = max(1, share // STATE)
-    size = share // groups
+    lax.fori_loop(1, chips, arrive, 0)
 
     def scan(k, held):
-        i = n - 1 - k if backward else k
+        i = chips - 1 - k if backward else k
         outbox[i] = held.astype(BF16)
 
-        @pl.when(i != me)
+        @pl.when(i != chip)
         def _():
-            out_copy(i, me).start()
+            f_copy(i, chip).start()
 
         grown = [
             held[g * size : (g + 1) * size] * decbox[i, g : g + 1, :] for g in range(groups)
@@ -316,44 +389,91 @@
         grown = grown[0] if groups == 1 else jnp.concatenate(grown, axis=0)
         return grown + inbox[i].astype(F32)
 
-    lax.fori_loop(0, n, scan, jnp.zeros((share, LANES), F32))
-    out_ref[rows_of(me, share), :] = outbox[me]
+    lax.fori_loop(0, chips, scan, jnp.zeros((share, LANES), F32))
+    fbox[rows_of(chip, share), :] = outbox[chip]
+    if not backward:
+        ring(1)
+
+    def landed(k, _):
+        peer = lax.rem(chip + k, chips)
+        f_copy(peer, peer).wait_recv()
+        return 0
+
+    lax.fori_loop(1, chips, landed, 0)
+    for h in range(HEADS):
+        rows = pl.ds(pl.multiple_of(core * half + h * STATE, STATE), STATE)
+        came = fbox[srows(h), :].astype(F32)
+        near = jnp.where(near_is_me, st_ref[rows, :].astype(F32), mate[srows(h), :].astype(F32))
+        later = scaled(neardec, came, h) + near
+        out_ref[rows, :] = jnp.where(near_is_me, came, later).astype(BF16)
+        other[srows(h), :] = jnp.where(near_is_me, later, came).astype(BF16)
+    last = remote(other, out_ref.at[rows_of(core, half), :], last_send, last_recv, partner)
+    last.start()
+    if not backward:
+        for step in range(2, cw_steps + 1):
+            ring(step)
+
+        def mate_block(k, _):
+            block = 2 * k + 1 - core
+            w_copy(block, pair_send, partner).wait_recv()
+            return 0
+
+        lax.fori_loop(0, chips, mate_block, 0)
+        for copy in sent:
+            copy.wait_send()
+        dec_mate.wait_send()
 
     def finish(k, _):
-        other = lax.rem(me + k, n)
-        out_copy(other, other).wait_recv()
-        out_copy(other, me).wait_send()
-        st_copy(other, me).wait_send()
-        if backward:
-            nt_copy(other, other).wait_recv()
-            nt_copy(other, me).wait_send()
-        else:
-            dec_copy(other, me).wait_send()
+        peer = lax.rem(chip + k, chips)
+        in_copy(peer, chip).wait_send()
+        f_copy(peer, chip).wait_send()
+        if not backward:
+            dec_copy(peer, chip).wait_send()
         return 0
 
-    lax.fori_loop(1, n, finish, 0)
+    lax.fori_loop(1, chips, finish, 0)
+    if backward:
+
+        def finish_nt(k, _):
+            peer = lax.rem(me + k, n)
+            nt_copy(peer, peer).wait_recv()
+            nt_copy(peer, me).wait_send()
+            return 0
+
+        lax.fori_loop(1, n, finish_nt, 0)
+    to_mate.wait_send()
+    last.wait()
     block_copy.wait()
 
 
 def exchange(n, backward, *operands):
+    chips = n // 2
     share = ROWS // n
-    outs = [jax.ShapeDtypeStruct((ROWS, LANES), BF16), jax.ShapeDtypeStruct((TOK, D), BF16)]
+    outs = [out_of(ROWS, LANES), out_of(TOK, D)]
     if backward:
-        outs.append(jax.ShapeDtypeStruct((n, INNER // n, 2 * TOK), BF16))
+        outs.append(out_of(n, INNER // n, 2 * TOK))
     else:
-        outs.append(jax.ShapeDtypeStruct((n, 8, LANES), F32))
+        outs += [
+            out_of(HEADS, LANES, dtype=F32), out_of(chips, 8, LANES, dtype=F32), out_of(n, INNER // n, D)
+        ]
     dma = pltpu.SemaphoreType.DMA
     vmem = pl.BlockSpec(memory_space=pltpu.VMEM)
+    sems = [dma((2,)), dma((2,)), dma((chips,)), dma((chips,)), dma((chips,)), dma((chips,)), dma, dma, dma, dma]
+    if backward:
+        sems += [dma((n,)), dma((n,))]
+    else:
+        sems += [dma((chips,)), dma((chips,)), dma((n,)), dma((n,)), dma((n,)), dma((n,))]
     return pl.pallas_call(
         functools.partial(exchange_kernel, n, backward),
         out_shape=outs,
         in_specs=[vmem] * len(operands),
-        out_specs=[vmem] * 3,
+        out_specs=[vmem] * len(outs),
         scratch_shapes=[
-            pltpu.VMEM((n, share, LANES), BF16),
-            pltpu.VMEM((n, share, LANES), BF16),
-            dma((n,)), dma((n,)), dma((n,)), dma((n,)), dma, dma, dma((n,)), dma((n,)),
-        ],
+            pltpu.VMEM((ROWS // 2, LANES), BF16), pltpu.VMEM((ROWS // 2, LANES), BF16),
+            pltpu.VMEM((chips, share, LANES), BF16), pltpu.VMEM((chips, share, LANES), BF16),
+            pltpu.VMEM((ROWS // 2, LANES), BF16), pltpu.VMEM((ROWS // 2, LANES), BF16),
+            pltpu.VMEM((chips, 8, LANES), F32),
+        ] + sems,
         compiler_params=pltpu.CompilerParams(
             collective_id=1 if backward else 0, has_side_effects=True, vmem_limit_bytes=VMEM_LIMIT
         ),
@@ -383,14 +503,12 @@
     proj_main, proj_state, step_raw, step_bias, decay_log, skip_scale, norm_gain, out_weight, grad_mixed
 ):
     n = lax.axis_size("seq")
-    share = ROWS // n
     spare = LANES - HEADS
     raw = jnp.pad(step_raw, ((0, 0), (0, 0), (0, spare)))
     bias, dlog, skip = (
         jnp.pad(v, (0, spare)).reshape(1, LANES) for v in (step_bias, decay_log, skip_scale)
     )
     gain = norm_gain.reshape(1, INNER)
-    whole_weight = lax.all_gather(out_weight, "seq", axis=0, tiled=True)
     whole_grad = lax.all_gather(grad_mixed, "seq", axis=0, tiled=True)
 
     main_x = pl.BlockSpec((1, TOK, INNER), lambda s: (s, 0, 0))
@@ -404,10 +522,11 @@
         out_shape=[out_of(2, state_rows, LANES), out_of(2, 1, LANES, dtype=F32)],
         compiler_params=PARAMS,
     )(proj_main, proj_state, raw, bias, dlog)
-    decays = dec[:, 0, :HEADS].reshape(2 * HEADS)
-    table = [[min(j * share // STATE + k, 2 * HEADS - 1) for k in range(8)] for j in range(n)]
-    decs = jnp.broadcast_to(decays[jnp.array(table)][:, :, None], (n, 8, LANES))
-    entering, grad_far, decbox = exchange(n, False, st.reshape(ROWS, LANES), decs, grad_mixed)
+    decs = jnp.broadcast_to(dec[:, 0, :HEADS, None], (2, HEADS, LANES)).reshape(2 * HEADS, LANES)
+    entering, grad_far, matedec, decbox, whole_weight = exchange(
+        n, False, st.reshape(ROWS, LANES), decs, grad_mixed, out_weight
+    )
+    whole_weight = whole_weight.reshape(INNER, D)
     entering = entering.reshape(2, state_rows, LANES)
 
     nt, so, gz, gy, de, gyy = pl.pallas_call(
@@ -434,7 +553,9 @@
         compiler_params=PARAMS,
     )(proj_main, proj_state, raw, bias, dlog, skip, gain, whole_weight, grad_mixed, grad_far, entering)
 
-    leaving, so_far, all_nt = exchange(n, True, de.reshape(ROWS, LANES), decbox, so[1], nt)
+    leaving, so_far, all_nt = exchange(
+        n, True, de.reshape(ROWS, LANES), decs, so[1], matedec, decbox, nt
+    )
     leaving = leaving.reshape(2, state_rows, LANES)
 
     grad_main, grad_state, grad_step = pl.pallas_call(

time: 218 us -> 207 us (0.950)
  waiting for transfers between devices: 9.36 us -> 0.68 us
    all_gather x1 -> x0, waiting for transfers between devices: 7.98 us -> none  [per_device(): whole_weight = lax.all_gather(out_weight, 'seq', axis=0, tiled=True)]
  transfers between devices with their start and end apart: 2 -> 1, of which waited for: 1 -> 0; matrix products, arithmetic and copies ran while one was open for 5% -> 4% of each run, Pallas kernels for 80% -> 84%
where the time goes in v2:
time: 207 us
  Pallas kernels  183 us (88%)
  between operations  14.1 us (7%)
  local copies, waits for them, and re-layouts  8.8 us (4%)
    pallas_call x2, Pallas kernels, exchange(): pl.pallas_call(functools.partial(exchange_kernel, n, backward), out_shape...  143 us
    pallas_call x1, Pallas kernels, per_device(): pl.pallas_call(middle_kernel, grid=(2,), in_specs=[strand_block(TOK, 2 *...  14.5 us
    pallas_call x1, Pallas kernels, per_device(): pl.pallas_call(last_kernel, grid=(2,), in_specs=[main_x, strand_block(TOK...  12.2 us
    pallas_call x1, Pallas kernels, per_device(): pl.pallas_call(functools.partial(weight_kernel, n), in_specs=[vmem] * 4,...  10.6 us
  transfers between devices with their start and end apart: 1, of which 0 were waited for; matrix products, arithmetic and copies ran while one was open for 4% of the time, Pallas kernels for 84%

profile of v2, /device:TPU:0, one launch (start us, length us, event | category | flops | bytes accessed | tf_op | source)
XLA Modules:
  0.0 206.9 jit_solution(4679196179141436825)
XLA Ops:
  7.2 0.0 all-gather.2.cloned.1.call-start
  7.2 0.7 all-gather.2.cloned.1.call-update
  7.9 0.8 copy.14
  8.7 0.7 pad.14.raw_ref
  9.4 1.3 pad_bitcast_fusion.1
  10.6 3.5 %shard_map.128 = (bf16[2,1024,128]{2,1,0:T(8,128)(2,1)}, f32[2,1,128]{2,1,0:T(1,128)}) custom-call(bf16[2,128,4096]{2,1,0:T(8,128)(2,1)} %x_ref.3, bf16[2,128,128]{2,1,0:T(8,128)(2,1)} %bc_ref.5, f32[2,128,128]{2,1,0:T(8,128)} %pad.14.raw_ref, f32[1,128]{1,0:T(1,128)} %get-tuple-element.55.bias_ref, f32[1,128]{1,0:T(1,128)} %get-tuple-element.54.dlog_ref), custom_call_target="tpu_custom_call" | custom-call | tf_op jit(solution)/shard_map/pallas_call | solution.py:517
  14.1 0.7 slice_reduce_fusion
  14.8 0.1 broadcast_in_dim.7
  14.9 0.7 broadcast_in_dim.8.refs_1_
  15.6 82.4 %shard_map.129 = (bf16[2048,128]{1,0:T(8,128)(2,1)}, bf16[128,1024]{1,0:T(8,128)(2,1)}, f32[16,128]{1,0:T(8,128)}, f32[8,8,128]{2,1,0:T(8,128)}, bf16[16,128,1024]{2,1,0:T(8,128)(2,1)}) custom-call(bf16[2048,128]{1,0:T(8,128)(2,1)} %bitcast.21, f32[32,128]{1,0:T(8,128)} %broadcast_in_dim.8.refs_1_, bf16[128,1024]{1,0:T(8,128)(2,1)} %gm_ref.1, ...), custom_call_target="tpu_custom_call" | custom-call | tf_op jit(solution)/shard_map/pallas_call | solution.py:466
  98.0 1.2 pad_bitcast_fusion.skip_ref
  99.2 14.5 %shard_map.130 = (bf16[2048,256]{1,0:T(8,128)(2,1)}, bf16[2,128,1024]{2,1,0:T(8,128)(2,1)}, bf16[2,128,2048]{2,1,0:T(8,128)(2,1)}, bf16[2,128,2048]{2,1,0:T(8,12...) custom-call(bf16[2,128,4096]{2,1,0:T(8,128)(2,1)} %x_ref.3, bf16[2,128,128]{2,1,0:T(8,128)(2,1)} %bc_ref.5, ...), custom_call_target="tpu_custom_call" | custom-call | tf_op jit(solution)/shard_map/pallas_call | solution.py:532
  113.7 1.9 slice_bitcast_fusion
  115.6 60.1 %shard_map.131 = (bf16[2048,128]{1,0:T(8,128)(2,1)}, bf16[128,1024]{1,0:T(8,128)(2,1)}, bf16[16,128,256]{2,1,0:T(8,128)(2,1)}) custom-call(bf16[2048,128]{1,0:T(8,128)(2,1)} %bitcast.22, f32[32,128]{1,0:T(8,128)} %broadcast_in_dim.8.refs_1_, bf16[128,1024]{1,0:T(8,128)(2,1)} %get-tuple-element.53.refs_2_, f32[16,128]{1,0:T(8,128)} %get-tuple-element.33.refs_3_, ...), custom_call_target="tpu_custom_call" | custom-call | tf_op jit(solution)/shard_map/pallas_call | solution.py:466
  175.7 12.2 %shard_map.133 = (bf16[2,128,4096]{2,1,0:T(8,128)(2,1)}, f32[2,128,128]{2,1,0:T(8,128)}, f32[2,128,128]{2,1,0:T(8,128)}) custom-call(bf16[2,128,4096]{2,1,0:T(8,128)(2,1)} %x_ref.3, bf16[2,128,2048]{2,1,0:T(8,128)(2,1)} %get-tuple-element.39.gz_ref, bf16[2,128,2048]{2,1,0:T(8,128)(2,1)} %get-tuple-element.40.gy_ref, bf16[2,128,128]{2,1,0:T(8,128)(2,1)} %bc_ref.5, ...), custom_call_target="tpu_custom_call" | custom-call | tf_op jit(solution)/shard_map/pallas_call | solution.py:561
  187.9 1.6 copy.15
  189.5 0.0 all-gather.2.cloned.1.call-done.gm_ref
  189.5 10.6 %shard_map.132 = (f32[128,1024]{1,0:T(8,128)}, bf16[128,1024]{1,0:T(8,128)(2,1)}) custom-call(bf16[16,128,256]{2,1,0:T(8,128)(2,1)} %get-tuple-element.36.nt_ref, bf16[2048,1024]{1,0:T(8,128)(2,1)} %all-gather.2.cloned.1.call-done.gm_ref, bf16[128,1024]{1,0:T(8,128)(2,1)} %get-tuple-element.52.so_ref, bf16[128,1024]{1,0:T(8,128)(2,1)} %get-tuple-element.37.som_ref), custom_call_target="tpu_custom_call" | custom-call | tf_op jit(solution)/shard_map/pallas_call | solution.py:578
Async XLA Ops:
  7.2 182.3 %all-gather.2.cloned.1.call-start = ((), (), s32[]{:S(2)}) async-start(), calls=%async_computation | async-start | bytes 4456448 | tf_op jit(solution)/shard_map/all_gather | solution.py:512
Sparse Core Ops, SparseCore 0:
  10.2 73.6 all-gather.1

commit v3 on v2

--- a/solution.py
+++ b/solution.py
@@ -49,7 +49,8 @@
     return jnp.concatenate(parts, axis=1)
 
 
-def steps(raw, bias, dlog):
+def steps(raw_t, bias, dlog):
+    raw = jnp.concatenate([raw_t, jnp.zeros((LANES - HEADS, TOK), F32)], axis=0).T
     arg = raw + bias
     size = jnp.maximum(arg, 0.0) + jnp.log1p(jnp.exp(-jnp.abs(arg)))
     rate = -jnp.exp(dlog) * size
@@ -75,7 +76,7 @@
     for h in range(HEADS):
         xw = (x_ref[0, :, head(h)].astype(F32) * weight[:, h : h + 1]).astype(BF16)
         st_ref[0, srows(h), :] = dot(b, xw, 0, 0).astype(BF16)
-    dec_ref[0] = jnp.exp(total)
+    dec_ref[0] = jnp.broadcast_to(jnp.exp(cum.T[:HEADS, TOK - 1 :]), (HEADS, LANES))
 
 
 def mixing(scores, mask, cum, cum_t, size_t, h):
@@ -190,20 +191,14 @@
     upper = (row <= col).astype(F32)
     grate = dot(upper, gcum, precision=HIGH) + gtotal
     gsize = xdx_s[...] / size - jnp.exp(dlog_ref[...]) * grate
-    gstep_ref[0] = gsize / (1.0 + jnp.exp(-arg))
+    gstep_ref[0] = (gsize / (1.0 + jnp.exp(-arg))).T[:HEADS]
 
 
 def weight_kernel(n, nt_ref, gm_ref, so_ref, som_ref, gw_ref, mixed_ref):
-    plain = jnp.zeros(gw_ref.shape, F32)
-    turned = jnp.zeros(gw_ref.shape, F32)
-
-    def body(i, held):
-        plain, turned = held
-        near = gm_ref[pl.ds(pl.multiple_of(i * TOK, TOK), TOK), :]
-        far = gm_ref[pl.ds(pl.multiple_of((n - 1 - i) * TOK, TOK), TOK), :]
-        return plain + dot(nt_ref[i, :, :TOK], near), turned + dot(nt_ref[i, :, TOK:], far)
-
-    plain, turned = lax.fori_loop(0, n, body, (plain, turned))
+    near = jnp.concatenate([nt_ref[i, :, :TOK] for i in range(n)], axis=1)
+    far = jnp.concatenate([nt_ref[n - 1 - i, :, TOK:] for i in range(n)], axis=1)
+    plain = dot(near, gm_ref[...])
+    turned = dot(far, gm_ref[...])
     row, col = grids()
     anti = (row + col == TOK - 1).astype(F32)
     count = D // TOK
@@ -212,7 +207,7 @@
         gw_ref[:, k * TOK : (k + 1) * TOK] = plain[:, k * TOK : (k + 1) * TOK] + dot(
             back, anti, precision=HIGH
         )
-    mixed_ref[...] = (so_ref[...].astype(F32) + flip_both(som_ref[...]).astype(F32)).astype(BF16)
+    mixed_ref[...] = (so_ref[0].astype(F32) + flip_both(som_ref[...]).astype(F32)).astype(BF16)
 
 
 def exchange_kernel(n, backward, *refs):
@@ -220,7 +215,7 @@
         (st_ref, dec_ref, block_ref, matedec, decbox, nt_ref, out_ref, gotblock_ref, gotnt_ref) = refs[:9]
         rest = refs[9:]
     else:
-        (st_ref, dec_ref, block_ref, w_ref, out_ref, gotblock_ref, matedec, decbox, wall_ref) = refs[:9]
+        (st_ref, dec_ref, g_ref, w_ref, out_ref, gall_ref, matedec, decbox, wall_ref) = refs[:9]
         rest = refs[9:]
     (mate, comb, inbox, outbox, fbox, other, decout), sems = rest[:7], rest[7:]
     (mate_send, mate_recv, in_send, in_recv, f_send, f_recv, last_send, last_recv, block_send, block_recv) = sems[:10]
@@ -279,18 +274,15 @@
             nt_ref.at[rows_of(to, inner), :], gotnt_ref.at[slot], extra[0].at[to], extra[1].at[slot], to
         )
 
-    block_copy = remote(block_ref, gotblock_ref, block_send, block_recv, n - 1 - me)
+    if backward:
+        block_copy = remote(block_ref.at[1], gotblock_ref, block_send, block_recv, n - 1 - me)
 
     if not backward:
-        w_recv, cw_send, ccw_send, pair_send = extra[2:]
         place = jnp.where(lax.rem(chip, 2) == 0, chip // 2, chips - 1 - chip // 2)
 
         def at(offset):
             pos = lax.rem(place + offset + 2 * chips, chips)
             return jnp.where(pos < chips // 2, 2 * pos, 2 * (chips - 1 - pos) + 1)
-
-        def w_copy(block, sems_, to):
-            return remote(wall_ref.at[block], wall_ref.at[block], sems_.at[block], w_recv.at[block], to)
 
         right, left = 2 * at(1) + core, 2 * at(-1) + core
         cw_steps = chips // 2
@@ -301,30 +293,28 @@
             copy.start()
             sent.append(copy)
 
+        def block_copy_of(which, block, lane, to):
+            whole, sems_ = ((wall_ref, extra[2:6]), (gall_ref, extra[6:10]))[which]
+            return remote(whole.at[block], whole.at[block], sems_[lane].at[block], sems_[3].at[block], to)
+
+        def ring_of(which, step):
+            for lane, count, sign, to in ((0, cw_steps, -1, right), (1, ccw_steps, 1, left)):
+                if step > count:
+                    continue
+                block = 2 * at(sign * step) + core
+                if step > 0:
+                    block_copy_of(which, block, lane, to).wait_recv()
+                if step < count:
+                    launch(block_copy_of(which, block, lane, to))
+                if step > 0 or lane == 0:
+                    launch(block_copy_of(which, block, 2, partner))
+
         def ring(step):
-            if step < cw_steps:
-                block = 2 * at(-step) + core
-                if step > 0:
-                    w_copy(block, cw_send, right).wait_recv()
-                launch(w_copy(block, cw_send, right))
-                if step > 0:
-                    launch(w_copy(block, pair_send, partner))
-            if step < ccw_steps:
-                block = 2 * at(step) + core
-                if step > 0:
-                    w_copy(block, ccw_send, left).wait_recv()
-                launch(w_copy(block, ccw_send, left))
-                launch(w_copy(block, pair_send, partner))
-            if step == cw_steps:
-                block = 2 * at(-step) + core
-                w_copy(block, cw_send, right).wait_recv()
-                launch(w_copy(block, pair_send, partner))
-            if step == ccw_steps:
-                block = 2 * at(step) + core
-                w_copy(block, ccw_send, left).wait_recv()
-                launch(w_copy(block, pair_send, partner))
+            ring_of(0, step)
+            ring_of(1, step)
 
         wall_ref[me] = w_ref[...]
+        gall_ref[me] = g_ref[...]
         ring(0)
 
     def scaled(dec, rows, h):
@@ -358,13 +348,14 @@
         return 0
 
     lax.fori_loop(1, chips, start_in, 0)
-    block_copy.start()
     inbox[chip] = comb[rows_of(chip, share), :]
     if backward:
+        block_copy.start()
         lax.fori_loop(1, n, lambda k, _: (nt_copy(lax.rem(me + k, n), me).start(), 0)[1], 0)
         gotnt_ref[me] = nt_ref[rows_of(me, inner), :]
     else:
         decbox[chip] = decout[chip]
+        ring(1)
 
     def arrive(k, _):
         peer = lax.rem(chip + k, chips)
@@ -391,8 +382,6 @@
 
     lax.fori_loop(0, chips, scan, jnp.zeros((share, LANES), F32))
     fbox[rows_of(chip, share), :] = outbox[chip]
-    if not backward:
-        ring(1)
 
     def landed(k, _):
         peer = lax.rem(chip + k, chips)
@@ -415,7 +404,8 @@
 
         def mate_block(k, _):
             block = 2 * k + 1 - core
-            w_copy(block, pair_send, partner).wait_recv()
+            block_copy_of(0, block, 2, partner).wait_recv()
+            block_copy_of(1, block, 2, partner).wait_recv()
             return 0
 
         lax.fori_loop(0, chips, mate_block, 0)
@@ -443,13 +433,14 @@
         lax.fori_loop(1, n, finish_nt, 0)
     to_mate.wait_send()
     last.wait()
-    block_copy.wait()
+    if backward:
+        block_copy.wait()
 
 
 def exchange(n, backward, *operands):
     chips = n // 2
     share = ROWS // n
-    outs = [out_of(ROWS, LANES), out_of(TOK, D)]
+    outs = [out_of(ROWS, LANES), out_of(TOK, D) if backward else out_of(n, TOK, D)]
     if backward:
         outs.append(out_of(n, INNER // n, 2 * TOK))
     else:
@@ -462,7 +453,7 @@
     if backward:
         sems += [dma((n,)), dma((n,))]
     else:
-        sems += [dma((chips,)), dma((chips,)), dma((n,)), dma((n,)), dma((n,)), dma((n,))]
+        sems += [dma((chips,)), dma((chips,))] + [dma((n,))] * 8
     return pl.pallas_call(
         functools.partial(exchange_kernel, n, backward),
         out_shape=outs,
@@ -504,12 +495,11 @@
 ):
     n = lax.axis_size("seq")
     spare = LANES - HEADS
-    raw = jnp.pad(step_raw, ((0, 0), (0, 0), (0, spare)))
+    raw = jnp.swapaxes(step_raw, 1, 2)
     bias, dlog, skip = (
         jnp.pad(v, (0, spare)).reshape(1, LANES) for v in (step_bias, decay_log, skip_scale)
     )
     gain = norm_gain.reshape(1, INNER)
-    whole_grad = lax.all_gather(grad_mixed, "seq", axis=0, tiled=True)
 
     main_x = pl.BlockSpec((1, TOK, INNER), lambda s: (s, 0, 0))
     row = fixed_block(1, LANES)
@@ -517,23 +507,25 @@
     st, dec = pl.pallas_call(
         local_state_kernel,
         grid=(2,),
-        in_specs=[main_x, strand_block(TOK, 2 * STATE), strand_block(TOK, LANES), row, row],
-        out_specs=[strand_block(state_rows, LANES), strand_block(1, LANES)],
-        out_shape=[out_of(2, state_rows, LANES), out_of(2, 1, LANES, dtype=F32)],
+        in_specs=[main_x, strand_block(TOK, 2 * STATE), strand_block(HEADS, TOK), row, row],
+        out_specs=[strand_block(state_rows, LANES), strand_block(HEADS, LANES)],
+        out_shape=[out_of(2, state_rows, LANES), out_of(2, HEADS, LANES, dtype=F32)],
         compiler_params=PARAMS,
     )(proj_main, proj_state, raw, bias, dlog)
-    decs = jnp.broadcast_to(dec[:, 0, :HEADS, None], (2, HEADS, LANES)).reshape(2 * HEADS, LANES)
-    entering, grad_far, matedec, decbox, whole_weight = exchange(
+    decs = dec.reshape(2 * HEADS, LANES)
+    entering, whole_grad, matedec, decbox, whole_weight = exchange(
         n, False, st.reshape(ROWS, LANES), decs, grad_mixed, out_weight
     )
     whole_weight = whole_weight.reshape(INNER, D)
+    grad_far = lax.dynamic_index_in_dim(whole_grad, n - 1 - lax.axis_index("seq"), 0, keepdims=False)
+    whole_grad = whole_grad.reshape(n * TOK, D)
     entering = entering.reshape(2, state_rows, LANES)
 
     nt, so, gz, gy, de, gyy = pl.pallas_call(
         middle_kernel,
         grid=(2,),
         in_specs=[
-            strand_block(TOK, 2 * INNER), strand_block(TOK, 2 * STATE), strand_block(TOK, LANES),
+            strand_block(TOK, 2 * INNER), strand_block(TOK, 2 * STATE), strand_block(HEADS, TOK),
             row, row, row, fixed_block(1, INNER), fixed_block(INNER, D), fixed_block(TOK, D),
             fixed_block(TOK, D), strand_block(state_rows, LANES),
         ],
@@ -554,7 +546,7 @@
     )(proj_main, proj_state, raw, bias, dlog, skip, gain, whole_weight, grad_mixed, grad_far, entering)
 
     leaving, so_far, all_nt = exchange(
-        n, True, de.reshape(ROWS, LANES), decs, so[1], matedec, decbox, nt
+        n, True, de.reshape(ROWS, LANES), decs, so, matedec, decbox, nt
     )
     leaving = leaving.reshape(2, state_rows, LANES)
 
@@ -563,12 +555,12 @@
         grid=(2,),
         in_specs=[
             main_x, strand_block(TOK, INNER), strand_block(TOK, INNER), strand_block(TOK, 2 * STATE),
-            strand_block(TOK, LANES), row, row, row, strand_block(state_rows, LANES),
+            strand_block(HEADS, TOK), row, row, row, strand_block(state_rows, LANES),
             strand_block(state_rows, LANES), strand_block(TOK, LANES),
         ],
-        out_specs=[strand_block(TOK, 2 * INNER), strand_block(TOK, 2 * STATE), strand_block(TOK, LANES)],
+        out_specs=[strand_block(TOK, 2 * INNER), strand_block(TOK, 2 * STATE), strand_block(HEADS, TOK)],
         out_shape=[
-            out_of(2, TOK, 2 * INNER), out_of(2, TOK, 2 * STATE, dtype=F32), out_of(2, TOK, LANES, dtype=F32),
+            out_of(2, TOK, 2 * INNER), out_of(2, TOK, 2 * STATE, dtype=F32), out_of(2, HEADS, TOK, dtype=F32),
         ],
         scratch_shapes=[pltpu.VMEM((TOK, LANES), F32)],
         compiler_params=PARAMS,
@@ -581,8 +573,8 @@
         out_specs=[vmem] * 2,
         out_shape=[out_of(INNER // n, D, dtype=F32), out_of(TOK, D)],
         compiler_params=PARAMS,
-    )(all_nt, whole_grad, so[0], so_far)
-    return mixed_out, grad_main, grad_state, grad_step[:, :, :HEADS], grad_weight
+    )(all_nt, whole_grad, so, so_far)
+    return mixed_out, grad_main, grad_state, jnp.swapaxes(grad_step, 1, 2), grad_weight
 
 
 def solution(mesh):

time: 207 us -> 170 us (0.82)
  Pallas kernels: 183 us -> 165 us
  between operations: 14.1 us -> 0.66 us
  local copies, waits for them, and re-layouts: 8.8 us -> 4.08 us
    pallas_call x2, Pallas kernels: 143 us -> 129 us  [exchange(): pl.pallas_call(functools.partial(exchange_kernel, n, backward), out_shape...]
    pallas_call x1, Pallas kernels: 10.6 us -> 5.44 us  [per_device(): pl.pallas_call(functools.partial(weight_kernel, n), in_specs=[vmem] * 4,...]
    unnamed x2 -> x0, local copies, waits for them, and re-layouts: 2.4 us -> none
  transfers between devices with their start and end apart: 1 -> 0, of which waited for: 0 -> 0; matrix products, arithmetic and copies ran while one was open for 4% -> 0% of each run, Pallas kernels for 84% -> 0%
where the time goes in v3:
time: 170 us
  Pallas kernels  165 us (97%)
  local copies, waits for them, and re-layouts  4.08 us (2%)
    pallas_call x2, Pallas kernels, exchange(): pl.pallas_call(functools.partial(exchange_kernel, n, backward), out_shape...  129 us
    pallas_call x1, Pallas kernels, per_device(): pl.pallas_call(middle_kernel, grid=(2,), in_specs=[strand_block(TOK, 2 *...  14.3 us
    pallas_call x1, Pallas kernels, per_device(): pl.pallas_call(last_kernel, grid=(2,), in_specs=[main_x, strand_block(TOK...  12.3 us
    pallas_call x1, Pallas kernels, per_device(): pl.pallas_call(functools.partial(weight_kernel, n), in_specs=[vmem] * 4,...  5.44 us
    pallas_call x1, Pallas kernels, per_device(): pl.pallas_call(local_state_kernel, grid=(2,), in_specs=[main_x, strand_bl...  3.59 us

profile of v3, /device:TPU:0, one launch (start us, length us, event | category | flops | bytes accessed | tf_op | source)
XLA Modules:
  0.0 169.6 jit_solution(10947581039765080018)
XLA Ops:
  0.6 1.2 pad_bitcast_fusion.skip_ref
  1.8 1.2 pad_bitcast_fusion.1
  3.0 3.6 %shard_map.128 = (bf16[2,1024,128]{2,1,0:T(8,128)(2,1)}, f32[2,16,128]{2,1,0:T(8,128)}) custom-call(bf16[2,128,4096]{2,1,0:T(8,128)(2,1)} %x_ref.3, bf16[2,128,128]{2,1,0:T(8,128)(2,1)} %bc_ref.5, f32[2,16,128]{2,1,0:T(8,128)} %bitcast.25, f32[1,128]{1,0:T(1,128)} %get-tuple-element.48.bias_ref, f32[1,128]{1,0:T(1,128)} %get-tuple-element.47.dlog_ref), custom_call_target="tpu_custom_call" | custom-call | tf_op jit(solution)/shard_map/pallas_call | solution.py:507
  6.6 72.4 %shard_map.129 = (bf16[2048,128]{1,0:T(8,128)(2,1)}, bf16[16,128,1024]{2,1,0:T(8,128)(2,1)}, f32[16,128]{1,0:T(8,128)}, f32[8,8,128]{2,1,0:T(8,128)}, bf16[16,128,1024]{2,1,0:T(8,128)(2,1)}) custom-call(bf16[2048,128]{1,0:T(8,128)(2,1)} %bitcast.23, f32[32,128]{1,0:T(8,128)} %bitcast.28, bf16[128,1024]{1,0:T(8,128)(2,1)} %gm_ref.1, bf16[128,1024]{1,0:T(8,128)(2,1)} %refs_3_.1), custom_call_target="tpu_custom_call" | custom-call | tf_op jit(solution)/shard_map/pallas_call | solution.py:457
  79.0 1.7 dynamic-slice_bitcast_fusion.gmm_ref
  80.7 14.3 %shard_map.130 = (bf16[2048,256]{1,0:T(8,128)(2,1)}, bf16[2,128,1024]{2,1,0:T(8,128)(2,1)}, bf16[2,128,2048]{2,1,0:T(8,128)(2,1)}, bf16[2,128,2048]{2,1,0:T(8,12...) custom-call(bf16[2,128,4096]{2,1,0:T(8,128)(2,1)} %x_ref.3, bf16[2,128,128]{2,1,0:T(8,128)(2,1)} %bc_ref.5, ...), custom_call_target="tpu_custom_call" | custom-call | tf_op jit(solution)/shard_map/pallas_call | solution.py:524
  95.0 56.9 %shard_map.131 = (bf16[2048,128]{1,0:T(8,128)(2,1)}, bf16[128,1024]{1,0:T(8,128)(2,1)}, bf16[16,128,256]{2,1,0:T(8,128)(2,1)}) custom-call(bf16[2048,128]{1,0:T(8,128)(2,1)} %bitcast.24, f32[32,128]{1,0:T(8,128)} %bitcast.29, bf16[2,128,1024]{2,1,0:T(8,128)(2,1)} %get-tuple-element.32.refs_2_.so_ref, f32[16,128]{1,0:T(8,128)} %get-tuple-element.33.refs_3_, ...), custom_call_target="tpu_custom_call" | custom-call | tf_op jit(solution)/shard_map/pallas_call | solution.py:457
  151.9 12.3 %shard_map.133 = (bf16[2,128,4096]{2,1,0:T(8,128)(2,1)}, f32[2,128,128]{2,1,0:T(8,128)}, f32[2,16,128]{2,1,0:T(8,128)}) custom-call(bf16[2,128,4096]{2,1,0:T(8,128)(2,1)} %x_ref.3, bf16[2,128,2048]{2,1,0:T(8,128)(2,1)} %get-tuple-element.39.gz_ref, bf16[2,128,2048]{2,1,0:T(8,128)(2,1)} %get-tuple-element.40.gy_ref, bf16[2,128,128]{2,1,0:T(8,128)(2,1)} %bc_ref.5, ...), custom_call_target="tpu_custom_call" | custom-call | tf_op jit(solution)/shard_map/pallas_call | solution.py:553
  164.2 5.4 %shard_map.132 = (f32[128,1024]{1,0:T(8,128)}, bf16[128,1024]{1,0:T(8,128)(2,1)}) custom-call(bf16[16,128,256]{2,1,0:T(8,128)(2,1)} %get-tuple-element.36.nt_ref, bf16[2048,1024]{1,0:T(8,128)(2,1)} %bitcast.18, bf16[2,128,1024]{2,1,0:T(8,128)(2,1)} %get-tuple-element.32.refs_2_.so_ref, bf16[128,1024]{1,0:T(8,128)(2,1)} %get-tuple-element.37.som_ref), custom_call_target="tpu_custom_call" | custom-call | tf_op jit(solution)/shard_map/pallas_call | solution.py:570

commit v4 on v3

--- a/solution.py
+++ b/solution.py
@@ -169,7 +169,7 @@
         m = (scores * w).astype(BF16)
         x, gy = x_ref[0, :, head(h)], gy_ref[0, :, head(h)]
         xf, gyf = x.astype(F32), gy.astype(F32)
-        lv, e = lv_ref[0, srows(h), :], e_ref[0, srows(h), :]
+        lv, e = lv_ref[srows(h), :], e_ref[srows(h), :]
         gscore += dot(gy, x, 1, 1) * w
         wcol = weight[:, h : h + 1]
         through = wcol * dot(b, lv)
@@ -212,8 +212,12 @@
 
 def exchange_kernel(n, backward, *refs):
     if backward:
-        (st_ref, dec_ref, block_ref, matedec, decbox, nt_ref, out_ref, gotblock_ref, gotnt_ref) = refs[:9]
-        rest = refs[9:]
+        (st_ref, dec_ref, block_ref, matedec, decbox, nt_ref) = refs[:6]
+        step_ins = refs[6:16]
+        gotblock_ref, gotnt_ref = refs[16:18]
+        step_outs = refs[18:21]
+        out_ref, xdx_s = refs[21:23]
+        rest = refs[23:]
     else:
         (st_ref, dec_ref, g_ref, w_ref, out_ref, gall_ref, matedec, decbox, wall_ref) = refs[:9]
         rest = refs[9:]
@@ -423,6 +427,20 @@
 
     lax.fori_loop(1, chips, finish, 0)
     if backward:
+        last.wait()
+        main_ref, gz_ref, gy_ref, bc_ref, raw_ref, bias_ref, dlog_ref, skip_ref, e_ref, gyy_ref = step_ins
+
+        def strand(s, _):
+            one = pl.ds(s, 1)
+            rows = rows_of(s, half)
+            last_kernel(
+                main_ref.at[one], gz_ref.at[one], gy_ref.at[one], bc_ref.at[one], raw_ref.at[one],
+                bias_ref, dlog_ref, skip_ref, e_ref.at[rows, :], out_ref.at[rows, :], gyy_ref.at[one],
+                *[ref.at[one] for ref in step_outs], xdx_s,
+            )
+            return 0
+
+        lax.fori_loop(0, 2, strand, 0)
 
         def finish_nt(k, _):
             peer = lax.rem(me + k, n)
@@ -432,19 +450,25 @@
 
         lax.fori_loop(1, n, finish_nt, 0)
     to_mate.wait_send()
-    last.wait()
     if backward:
         block_copy.wait()
+    else:
+        last.wait()
 
 
 def exchange(n, backward, *operands):
     chips = n // 2
     share = ROWS // n
-    outs = [out_of(ROWS, LANES), out_of(TOK, D) if backward else out_of(n, TOK, D)]
+    scratch = []
     if backward:
-        outs.append(out_of(n, INNER // n, 2 * TOK))
+        outs = [
+            out_of(TOK, D), out_of(n, INNER // n, 2 * TOK), out_of(2, TOK, 2 * INNER),
+            out_of(2, TOK, 2 * STATE, dtype=F32), out_of(2, HEADS, TOK, dtype=F32),
+        ]
+        scratch = [pltpu.VMEM((ROWS, LANES), BF16), pltpu.VMEM((TOK, LANES), F32)]
     else:
-        outs += [
+        outs = [
+            out_of(ROWS, LANES), out_of(n, TOK, D),
             out_of(HEADS, LANES, dtype=F32), out_of(chips, 8, LANES, dtype=F32), out_of(n, INNER // n, D)
         ]
     dma = pltpu.SemaphoreType.DMA
@@ -459,7 +483,7 @@
         out_shape=outs,
         in_specs=[vmem] * len(operands),
         out_specs=[vmem] * len(outs),
-        scratch_shapes=[
+        scratch_shapes=scratch + [
             pltpu.VMEM((ROWS // 2, LANES), BF16), pltpu.VMEM((ROWS // 2, LANES), BF16),
             pltpu.VMEM((chips, share, LANES), BF16), pltpu.VMEM((chips, share, LANES), BF16),
             pltpu.VMEM((ROWS // 2, LANES), BF16), pltpu.VMEM((ROWS // 2, LANES), BF16),
@@ -545,26 +569,10 @@
         compiler_params=PARAMS,
     )(proj_main, proj_state, raw, bias, dlog, skip, gain, whole_weight, grad_mixed, grad_far, entering)
 
-    leaving, so_far, all_nt = exchange(
-        n, True, de.reshape(ROWS, LANES), decs, so, matedec, decbox, nt
+    so_far, all_nt, grad_main, grad_state, grad_step = exchange(
+        n, True, de.reshape(ROWS, LANES), decs, so, matedec, decbox, nt,
+        proj_main, gz, gy, proj_state, raw, bias, dlog, skip, entering.reshape(ROWS, LANES), gyy,
     )
-    leaving = leaving.reshape(2, state_rows, LANES)
-
-    grad_main, grad_state, grad_step = pl.pallas_call(
-        last_kernel,
-        grid=(2,),
-        in_specs=[
-            main_x, strand_block(TOK, INNER), strand_block(TOK, INNER), strand_block(TOK, 2 * STATE),
-            strand_block(HEADS, TOK), row, row, row, strand_block(state_rows, LANES),
-            strand_block(state_rows, LANES), strand_block(TOK, LANES),
-        ],
-        out_specs=[strand_block(TOK, 2 * INNER), strand_block(TOK, 2 * STATE), strand_block(HEADS, TOK)],
-        out_shape=[
-            out_of(2, TOK, 2 * INNER), out_of(2, TOK, 2 * STATE, dtype=F32), out_of(2, HEADS, TOK, dtype=F32),
-        ],
-        scratch_shapes=[pltpu.VMEM((TOK, LANES), F32)],
-        compiler_params=PARAMS,
-    )(proj_main, gz, gy, proj_state, raw, bias, dlog, skip, entering, leaving, gyy)
 
     vmem = pl.BlockSpec(memory_space=pltpu.VMEM)
     grad_weight, mixed_out = pl.pallas_call(

time: 170 us -> 173 us (1.018)
  local copies, waits for them, and re-layouts: 4.08 us -> 6.76 us
    pallas_call x1 -> x0, Pallas kernels: 12.3 us -> none  [per_device(): pl.pallas_call(last_kernel, grid=(2,), in_specs=[main_x, strand_block(TOK...]
    pallas_call x2, Pallas kernels: 129 us -> 141 us  [exchange(): pl.pallas_call(functools.partial(exchange_kernel, n, backward), out_shape...]
    unnamed x0 -> x9, local copies, waits for them, and re-layouts: none -> 2.59 us
where the time goes in v4:
time: 173 us; the launch traced here: 172 us
  Pallas kernels  165 us (95%)
  local copies, waits for them, and re-layouts  6.76 us (4%)
    pallas_call x2, Pallas kernels, exchange(): pl.pallas_call(functools.partial(exchange_kernel, n, backward), out_shape...  141 us
    pallas_call x1, Pallas kernels, per_device(): pl.pallas_call(middle_kernel, grid=(2,), in_specs=[strand_block(TOK, 2 *...  14.3 us
    pallas_call x1, Pallas kernels, per_device(): pl.pallas_call(functools.partial(weight_kernel, n), in_specs=[vmem] * 4,...  5.59 us
    pallas_call x1, Pallas kernels, per_device(): pl.pallas_call(local_state_kernel, grid=(2,), in_specs=[main_x, strand_bl...  3.63 us

profile of v4, /device:TPU:0, one launch (start us, length us, event | category | flops | bytes accessed | tf_op | source)
XLA Modules:
  0.0 172.3 jit_solution(17104368028976074794)
XLA Ops:
  0.6 1.2 pad_bitcast_fusion.skip_ref.refs_13_
  1.9 1.3 pad_bitcast_fusion.1
  3.1 3.6 %shard_map.128 = (bf16[2,1024,128]{2,1,0:T(8,128)(2,1)}, f32[2,16,128]{2,1,0:T(8,128)}) custom-call(bf16[2,128,4096]{2,1,0:T(8,128)(2,1)} %refs_6_.1, bf16[2,128,128]{2,1,0:T(8,128)(2,1)} %refs_9_.1, f32[2,16,128]{2,1,0:T(8,128)} %bitcast.22, f32[1,128]{1,0:T(1,128)} %get-tuple-element.46.bias_ref.refs_11_, f32[1,128]{1,0:T(1,128)} %get-tuple-element.45.dlog_ref.refs_12_), custom_call_target="tpu_custom_call" | custom-call | tf_op jit(solution)/shard_map/pallas_call | solution.py:531
  6.8 72.4 %shard_map.129 = (bf16[2048,128]{1,0:T(8,128)(2,1)}, bf16[16,128,1024]{2,1,0:T(8,128)(2,1)}, f32[16,128]{1,0:T(8,128)}, f32[8,8,128]{2,1,0:T(8,128)}, bf16[16,128,1024]{2,1,0:T(8,128)(2,1)}) custom-call(bf16[2048,128]{1,0:T(8,128)(2,1)} %bitcast.21, f32[32,128]{1,0:T(8,128)} %bitcast.25, bf16[128,1024]{1,0:T(8,128)(2,1)} %gm_ref.1, bf16[128,1024]{1,0:T(8,128)(2,1)} %refs_3_.1), custom_call_target="tpu_custom_call" | custom-call | tf_op jit(solution)/shard_map/pallas_call | solution.py:481
  79.2 1.7 dynamic-slice_bitcast_fusion.gmm_ref
  80.9 14.3 %shard_map.130 = (bf16[2048,256]{1,0:T(8,128)(2,1)}, bf16[2,128,1024]{2,1,0:T(8,128)(2,1)}, bf16[2,128,2048]{2,1,0:T(8,128)(2,1)}, bf16[2,128,2048]{2,1,0:T(8,12...) custom-call(bf16[2,128,4096]{2,1,0:T(8,128)(2,1)} %refs_6_.1, bf16[2,128,128]{2,1,0:T(8,128)(2,1)} %refs_9_.1, ...), custom_call_target="tpu_custom_call" | custom-call | tf_op jit(solution)/shard_map/pallas_call | solution.py:548
  95.2 68.9 %shard_map.131 = (bf16[128,1024]{1,0:T(8,128)(2,1)}, bf16[16,128,256]{2,1,0:T(8,128)(2,1)}, bf16[2,128,4096]{2,1,0:T(8,128)(2,1)}, f32[2,128,128]{2,1,0:T(8,128)}, f32[2,16,128]{2,1,0:T(8,128)}) custom-call(bf16[2048,128]{1,0:T(8,128)(2,1)} %bitcast.20, f32[32,128]{1,0:T(8,128)} %bitcast.26, bf16[2,128,1024]{2,1,0:T(8,128)(2,1)} %get-tuple-element.31.refs_2_.so_ref, ...), custom_call_target="tpu_custom_call" | custom-call | tf_op jit(solution)/shard_map/pallas_call | solution.py:481
  164.1 0.0 copy-start
  164.1 0.0 copy-start.1
  164.1 0.0 copy-start.2
  164.1 5.6 %shard_map.132 = (f32[128,1024]{1,0:T(8,128)}, bf16[128,1024]{1,0:T(8,128)(2,1)}) custom-call(bf16[16,128,256]{2,1,0:T(8,128)(2,1)} %get-tuple-element.38.nt_ref, bf16[2048,1024]{1,0:T(8,128)(2,1)} %bitcast.17, bf16[2,128,1024]{2,1,0:T(8,128)(2,1)} %get-tuple-element.31.refs_2_.so_ref, bf16[128,1024]{1,0:T(8,128)(2,1)} %get-tuple-element.39.som_ref), custom_call_target="tpu_custom_call" | custom-call | tf_op jit(solution)/shard_map/pallas_call | solution.py:578
  169.7 0.0 copy-done
  169.7 1.3 copy.17
  171.0 0.0 copy-done.1
  171.0 0.7 copy.18
  171.7 0.0 copy-done.2
  171.7 0.6 copy.19
Async XLA Ops:
  164.1 5.6 %copy-start = (bf16[2,128,4096]{2,1,0:T(8,128)(2,1)S(1)}, bf16[2,128,4096]{2,1,0:T(8,128)(2,1)}, u32[]{:S(2)}) copy-start(bf16[2,128,4096]{2,1,0:T(8,128)(2,1)} %get-tuple-element.53) | copy-start | bytes 6291460
  164.1 6.9 %copy-start.1 = (f32[2,128,128]{2,1,0:T(8,128)S(1)}, f32[2,128,128]{2,1,0:T(8,128)}, u32[]{:S(2)}) copy-start(f32[2,128,128]{2,1,0:T(8,128)} %get-tuple-element.54) | copy-start | bytes 393220
  164.1 7.6 %copy-start.2 = (f32[2,16,128]{2,1,0:T(8,128)S(1)}, f32[2,16,128]{2,1,0:T(8,128)}, u32[]{:S(2)}) copy-start(f32[2,16,128]{2,1,0:T(8,128)} %get-tuple-element.43) | copy-start | bytes 49156
